TPU v7x, 256 devices: a whole 4x4x8 slice. The times are simulated.
256 devices in a mesh: head: 16 (over z, x_lo), blk: 16 (over x_hi, y, core).
Axes of the slice: x: 4 (x_hi: 2, x_lo: 2; x = x_hi * 2 + x_lo), y: 4, z: 8, core: 2. Of those that a mesh axis runs over, the one named last changes fastest.
Arguments:
- qkv: bfloat16 [16, 2048, 6144], P('blk', 'head'), may hold values from -9 to 9
- query_blocks: int32 [64], P('blk'), may hold values from 0 to 255, as said below
- out_weight: bfloat16 [2048, 3072], P('head')
- mod_shift: float32 [3072], replicated, may hold values from -3 to 3
- mod_scale: float32 [3072], replicated, may hold values from -3 to 3
- final_weight: bfloat16 [3072, 64], replicated, may hold values from -0.109375 to 0.109375
- final_bias: float32 [64], replicated, may hold values from -3 to 3
- conv_in_weight: bfloat16 [3, 3, 3, 16, 512], replicated, may hold values from -0.3125 to 0.3125
- conv_in_bias: float32 [512], replicated, may hold values from -3 to 3
- conv_weight: bfloat16 [3, 3, 3, 512, 512], P(None, None, None, None, 'head'), may hold values from -0.0546875 to 0.0546875
- conv_bias: float32 [512], replicated, may hold values from -3 to 3
Outputs:
- vae_features: bfloat16 [8, 64, 64, 512], P(None, 'blk', 'head')
Inputs may be any that keep to these rules, and one draw needn't show every extreme that they name: `query_blocks`: entry i names a block of 128 token rows among the 16 blocks held by index i // 4 of blk, that is from 16 * (i // 4) to 16 * (i // 4 + 1) - 1; the 4 entries of one index of blk are distinct, one from each run of 4 blocks, in any order.
All inputs are finite; a program needn't handle non-finite values.
Results may differ from a plain program's by a relative error of at most 0.023.
Values may be sent and summed in bfloat16 or wider, within the bound.
No kernel may reach another device: no remote copies, remote signals or barrier semaphores. Data moves between devices by JAX's collectives and lax.ppermute only.
A program may use at most 192 MiB of HBM per device.

v0:
```python
import math

import jax
import jax.numpy as jnp
from jax import lax
from jax.sharding import PartitionSpec as P

HEADS = 16
HD = 128
LAT = 16
QBLK = 128
TF = 8
TH = 2
TW = 2


norm_eps = 1e-06


def with_halo(cells, sides, width):
    for axis, dim in sides:
        count = lax.axis_size(axis)
        ends = count - 1
        head = lax.slice_in_dim(cells, 0, width, axis=dim)
        tail = lax.slice_in_dim(cells, cells.shape[dim] - width, cells.shape[dim], axis=dim)
        cells = jnp.concatenate(
            [
                lax.ppermute(tail, axis, [(i, (i + 1) % count) for i in range(ends)]),
                cells,
                lax.ppermute(head, axis, [((i + 1) % count, i) for i in range(ends)]),
            ],
            axis=dim,
        )
    return cells


def front_pad(field):
    return jnp.concatenate([field[:1], field[:1], field], axis=0)


def convolve(padded, weight):
    frames = padded.shape[0] - 2
    height = padded.shape[1] - 2
    breadth = padded.shape[2] - 2
    summed = jnp.zeros((frames, height, breadth, weight.shape[4]), jnp.float32)
    for tap_time in range(3):
        for tap_row in range(3):
            for tap_col in range(3):
                window = padded[
                    tap_time : tap_time + frames,
                    tap_row : tap_row + height,
                    tap_col : tap_col + breadth,
                ]
                summed = summed + jnp.einsum(
                    "thwc,co->thwo",
                    window,
                    weight[tap_time, tap_row, tap_col],
                    preferred_element_type=jnp.float32,
                )
    return summed


def shards(
    qkv,
    query_blocks,
    out_weight,
    mod_shift,
    mod_scale,
    final_weight,
    final_bias,
    conv_in_weight,
    conv_in_bias,
    conv_weight,
    conv_bias,
):
    head_count = lax.axis_size("head")
    local_heads = HEADS // head_count
    tok_count = qkv.shape[1]
    sectioned = qkv.reshape(tok_count, 3, head_count, local_heads, HD)
    shard_rows = tok_count * head_count
    per_shard = shard_rows // QBLK
    chosen = query_blocks % per_shard
    inverse_root = 1.0 / math.sqrt(HD)
    mixed = lax.all_to_all(sectioned, "head", split_axis=2, concat_axis=0, tiled=True)
    items = mixed.shape[3]
    query_all = mixed[:, 0, 0].reshape(per_shard, QBLK, items, HD)
    queries = jnp.take(query_all, chosen, axis=0).reshape(-1, items, HD)
    row_count = queries.shape[0]
    start_state = (
        jnp.full((items, row_count), -1e30, jnp.float32),
        jnp.zeros((items, row_count), jnp.float32),
        jnp.zeros((items, row_count, HD), jnp.float32),
    )
    state = start_state
    key_rows = lax.all_gather(mixed[:, 1, 0], "blk", axis=0, tiled=True)
    value_rows = lax.all_gather(mixed[:, 2, 0], "blk", axis=0, tiled=True)
    block_rows = math.gcd(1024, key_rows.shape[0])
    key_blocks = key_rows.reshape(-1, block_rows, items, HD)
    value_blocks = value_rows.reshape(-1, block_rows, items, HD)

    def absorb_block(running, pair):
        highest, totals, accum = running
        key_block, value_block = pair
        scores = (
            jnp.einsum("qhd,khd->hqk", queries, key_block, preferred_element_type=jnp.float32)
            * inverse_root
        )
        new_high = jnp.maximum(highest, jnp.max(scores, axis=2))
        weights = jnp.exp(scores - new_high[:, :, None])
        fading = jnp.exp(highest - new_high)
        totals = totals * fading + jnp.sum(weights, axis=2)
        accum = accum * fading[:, :, None] + jnp.einsum(
            "hqk,khd->hqd",
            weights.astype(jnp.bfloat16),
            value_block,
            preferred_element_type=jnp.float32,
        )
        return ((new_high, totals, accum), None)

    state, unused = lax.scan(absorb_block, state, (key_blocks, value_blocks))
    highest, totals, accum = state
    result = (accum / totals[:, :, None]).astype(jnp.bfloat16)
    attended = jnp.transpose(result, (1, 0, 2))[:, None]
    query_count = attended.shape[0]
    flat_rows = attended.reshape(query_count, local_heads * HD)
    projected = lax.psum_scatter(
        jnp.dot(flat_rows, out_weight, preferred_element_type=jnp.float32).astype(jnp.bfloat16),
        "head",
        scatter_dimension=0,
        tiled=True,
    ).astype(jnp.float32)
    average = jnp.mean(projected, axis=1, keepdims=True)
    centred = projected - average
    spread = jnp.mean(centred * centred, axis=1, keepdims=True)
    normed = centred * lax.rsqrt(spread + norm_eps)
    modulated = (normed * (1.0 + mod_scale) + mod_shift).astype(jnp.bfloat16)
    patches = (
        jnp.dot(modulated, final_weight, preferred_element_type=jnp.float32) + final_bias
    ).astype(jnp.bfloat16)
    latent = patches.reshape(TF, TH, TW, LAT, 2, 2)
    latent = jnp.transpose(latent, (0, 1, 4, 2, 5, 3)).reshape(TF, 2 * TH, 2 * TW, LAT)
    rimmed = with_halo(latent, (("head", 2), ("blk", 1)), 1)
    hidden = convolve(front_pad(rimmed), conv_in_weight) + conv_in_bias
    active = jax.nn.silu(hidden).astype(jnp.bfloat16)
    ready = with_halo(active, (("head", 2), ("blk", 1)), 1)
    padded = front_pad(ready)
    return (
        convolve(padded, lax.all_gather(conv_weight, "head", axis=4, tiled=True)) + conv_bias
    ).astype(jnp.bfloat16)


def solution(mesh):
    in_specs = (
        P("blk", "head", None),
        P("blk"),
        P("head", None),
        P(),
        P(),
        P(),
        P(),
        P(),
        P(),
        P(None, None, None, None, "head"),
        P(),
    )
    out_specs = P(None, "blk", "head", None)
    return jax.shard_map(shards, mesh=mesh, in_specs=in_specs, out_specs=out_specs, check_vma=False)
```

profile of v0, /device:TPU:4, one launch (start us, length us, event | category | flops | bytes accessed | tf_op | source)
XLA Modules:
  0.0 734.2 jit_solution(15238746121837491629)
XLA Ops:
  6.5 2.7 copy.54
  9.2 1.9 copy.55
  11.2 48.6 %all_to_all.18 = bf16[128,3,16,1,128]{4,0,1,3,2:T(8,128)(2,1)S(1)} all-to-all(bf16[128,3,16,1,128]{4,0,1,3,2:T(8,128)(2,1)S(1)} %copy.55), channel_id=1, replica_groups=mesh['head'=16,'blk'=16] {'head'}, dimensions={2} | all-to-all | bytes 3145728 | tf_op jit(solution)/shard_map/all_to_all | solution.py:84
  62.8 71.5 %all-gather.10.cloned.1.call-done = bf16[32768,1,1,1,128]{4,0,3,2,1:T(8,128)(2,1)} async-done(((bf16[2048,1,1,1,128]{4,0,3,2,1:T(8,128)(2,1)}), bf16[32768,1,1,1,128]{4,0,3,2,1:T(8,128)(2,1)}) %all-gather.10.cloned.1.call-update) | async-done | bytes 8388624 | tf_op jit(solution)/shard_map/all_gather | solution.py:96
  134.3 78.6 %all-gather.8.cloned.1.call-done = bf16[32768,1,1,1,128]{4,0,3,2,1:T(8,128)(2,1)} async-done(((bf16[2048,1,1,1,128]{4,0,3,2,1:T(8,128)(2,1)}), bf16[32768,1,1,1,128]{4,0,3,2,1:T(8,128)(2,1)}) %all-gather.8.cloned.1.call-update) | async-done | bytes 8388624 | tf_op jit(solution)/shard_map/all_gather | solution.py:95
  212.9 107.2 %while.15 = (s32[]{:T(128)}, f32[1,512]{1,0:T(1,128)S(1)}, f32[1,512]{1,0:T(1,128)S(1)}, f32[1,512,128]{2,1,0:T(8,128)S(1)}, bf16[32,1024,1,128]{3,1,2,0:T(8,128...) while((s32[]{:T(128)}, f32[1,512]{1,0:T(1,128)S(1)}, ...), condition=%wide.region_3.4_spmd.clone, body=%wide.region_0.3_spmd.clone.sunk | while | flops 272828928 | bytes 7505001 | solution.py:120
  214.8 1.5 fusion.189
  218.1 1.5 fusion.189
  221.5 1.5 fusion.189
  224.8 1.5 fusion.189
  228.2 1.5 fusion.189
  231.5 1.5 fusion.189
  234.9 1.5 fusion.189
  238.2 1.5 fusion.189
  241.6 1.5 fusion.189
  244.9 1.5 fusion.189
  320.2 2.7 convolution_convert_fusion
  323.5 81.8 %reduce-scatter.2.cloned.1.call-done = bf16[32,3072]{1,0:T(8,128)(2,1)} async-done(((bf16[512,3072]{1,0:T(8,128)(2,1)}), bf16[32,3072]{1,0:T(8,128)(2,1)}) %reduce-scatter.2.cloned.1.call-update) | async-done | bytes 196624 | tf_op jit(solution)/shard_map/reduce_scatter | solution.py:126
  409.8 1.9 collective-permute-start
  413.3 4.1 collective-permute-done.1
  417.3 1.9 collective-permute-start.2
  419.3 7.3 collective-permute-start.3
  426.7 4.0 collective-permute-done.2
  435.1 5.7 collective-permute-start.4
  443.0 4.9 collective-permute-done.5
  447.8 1.9 collective-permute-start.6
  449.8 7.4 %collective-permute-start.7 = (bf16[8,1,6,512]{3,0,2,1:T(8,128)(2,1)S(1)}, bf16[8,1,6,512]{3,0,2,1:T(8,128)(2,1)S(1)}, u32[]{:S(2)}, u32[]{:S(2)}) collective-permute-start(bf16[8,1,6,512]{3,0,2,1:T(8,128)(2,1)S(1)} %get-tuple-element.114), channel_id=1, source_target_pairs={{1,0},{2,1},{3,2},{4,3},{5,4},{6,5},{7,6},{8,7},{9,8},{10,9},{11,1... | collective-permute-start | bytes 147464 | tf_op jit(solution)/shard_map/ppermute | solution.py:30
  457.9 1.8 collective-permute-done.7
  460.3 244.6 %all-gather.6.cloned.1.call-done = bf16[3,3,3,512,512]{3,4,2,1,0:T(8,128)(2,1)} async-done(((bf16[3,3,3,512,32]{3,4,2,1,0:T(8,128)(2,1)}), bf16[3,3,3,512,512]{3,4,2,1,0:T(8,128)(2,1)}) %all-gather.6.cloned.1.call-update) | async-done | bytes 14155792 | tf_op jit(solution)/shard_map/all_gather | solution.py:148
  704.9 1.5 fusion.42
  706.4 1.7 fusion.41
  708.1 1.8 fusion.40
  (296 shorter events, 125.8 us)
Async XLA Ops:
  6.5 313.7 %copy-start = (bf16[128,3072]{1,0:T(8,128)(2,1)S(1)}, bf16[128,3072]{1,0:T(8,128)(2,1)}, u32[]{:S(2)}) copy-start(bf16[128,3072]{1,0:T(8,128)(2,1)} %param.15) | copy-start | bytes 2359300
  6.5 55.4 %copy-start.8 = (s32[4]{0:T(128)S(1)}, s32[4]{0:T(128)}, u32[]{:S(2)}) copy-start(s32[4]{0:T(128)} %param.14) | copy-start | bytes 52
  6.5 127.7 %all-gather.10.cloned.1.call-start = ((), (), s32[]{:S(2)}) async-start(), calls=%async_computation.5 | async-start | bytes 8912896 | tf_op jit(solution)/shard_map/all_gather | solution.py:96
  61.1 151.8 %all-gather.8.cloned.1.call-start = ((), (), s32[]{:S(2)}) async-start(), calls=%async_computation.4 | async-start | bytes 8912896 | tf_op jit(solution)/shard_map/all_gather | solution.py:95
  61.9 343.4 %reduce-scatter.2.cloned.1.call-start = ((), (), s32[]{:S(2)}) async-start(), calls=%async_computation.2 | async-start | bytes 3342336 | tf_op jit(solution)/shard_map/reduce_scatter | solution.py:126
  320.2 3.3 copy-start.3
  320.2 87.4 %copy-start.5 = (bf16[3072,64]{0,1:T(8,128)(2,1)S(1)}, bf16[3072,64]{0,1:T(8,128)(2,1)}, u32[]{:S(2)}) copy-start(bf16[3072,64]{0,1:T(8,128)(2,1)} %param.18) | copy-start | bytes 1179652
  320.2 87.4 %copy-start.6 = (f32[3072]{0:T(1024)S(1)}, f32[3072]{0:T(1024)}, u32[]{:S(2)}) copy-start(f32[3072]{0:T(1024)} %param.16) | copy-start | bytes 36868
  320.2 87.4 %copy-start.9 = (f32[64]{0:T(128)S(1)}, f32[64]{0:T(128)}, u32[]{:S(2)}) copy-start(f32[64]{0:T(128)} %param.19) | copy-start | bytes 772
  320.2 92.9 %copy-start.2 = (bf16[3,3,3,16,512]{4,3,2,1,0:T(8,128)(2,1)S(1)}, bf16[3,3,3,16,512]{4,3,2,1,0:T(8,128)(2,1)}, u32[]{:S(2)}) copy-start(bf16[3,3,3,16,512]{4,3,2,1,0:T(8,128)(2,1)} %param.20) | copy-start | bytes 1327108
  322.9 381.9 %all-gather.6.cloned.1.call-start = ((), (), s32[]{:S(2)}) async-start(), calls=%async_computation.3 | async-start | bytes 15040512 | tf_op jit(solution)/shard_map/all_gather | solution.py:148
  323.5 111.4 %copy-start.7 = (f32[512]{0:T(512)S(1)}, f32[512]{0:T(512)}, u32[]{:S(2)}) copy-start(f32[512]{0:T(512)} %param.21) | copy-start | bytes 6148
  409.8 3.4 collective-permute-start
  411.8 5.5 collective-permute-start.1
  417.3 13.4 %collective-permute-start.2 = (bf16[8,1,6,16]{3,0,2,1:T(8,128)(2,1)S(1)}, bf16[8,1,6,16]{3,0,2,1:T(8,128)(2,1)S(1)}, u32[]{:S(2)}, u32[]{:S(2)}) collective-permute-start(bf16[8,1,6,16]{3,0,2,1:T(8,128)(2,1)S(1)} %get-tuple-element.117), channel_id=1, source_target_pairs={{0,1},{1,2},{2,3},{3,4},{4,5},{5,6},{6,7},{7,8},{8,9},{9,10},{10,1... | collective-permute-start | bytes 4616 | tf_op jit(solution)/shard_map/ppermute | solution.py:28
  419.3 11.4 %collective-permute-start.3 = (bf16[8,1,6,16]{3,0,2,1:T(8,128)(2,1)S(1)}, bf16[8,1,6,16]{3,0,2,1:T(8,128)(2,1)S(1)}, u32[]{:S(2)}, u32[]{:S(2)}) collective-permute-start(bf16[8,1,6,16]{3,0,2,1:T(8,128)(2,1)S(1)} %get-tuple-element.118), channel_id=1, source_target_pairs={{1,0},{2,1},{3,2},{4,3},{5,4},{6,5},{7,6},{8,7},{9,8},{10,9},{11,1... | collective-permute-start | bytes 4616 | tf_op jit(solution)/shard_map/ppermute | solution.py:30
  435.1 7.8 %collective-permute-start.4 = (bf16[8,4,1,512]{3,0,2,1:T(8,128)(2,1)S(1)}, bf16[8,4,1,512]{3,0,2,1:T(8,128)(2,1)S(1)}, u32[]{:S(2)}, u32[]{:S(2)}) collective-permute-start(bf16[8,4,1,512]{3,0,2,1:T(8,128)(2,1)S(1)} %get-tuple-element.115), channel_id=1, source_target_pairs={{0,16},{16,32},{32,48},{48,64},{64,80},{80,96},{96,112},{112,128},... | collective-permute-start | bytes 98312 | tf_op jit(solution)/shard_map/ppermute | solution.py:28
  440.9 6.9 collective-permute-start.5
  447.8 10.0 %collective-permute-start.6 = (bf16[8,1,6,512]{3,0,2,1:T(8,128)(2,1)S(1)}, bf16[8,1,6,512]{3,0,2,1:T(8,128)(2,1)S(1)}, u32[]{:S(2)}, u32[]{:S(2)}) collective-permute-start(bf16[8,1,6,512]{3,0,2,1:T(8,128)(2,1)S(1)} %get-tuple-element.113), channel_id=1, source_target_pairs={{0,1},{1,2},{2,3},{3,4},{4,5},{5,6},{6,7},{7,8},{8,9},{9,10},{10,1... | collective-permute-start | bytes 147464 | tf_op jit(solution)/shard_map/ppermute | solution.py:28
  449.8 9.9 %collective-permute-start.7 = (bf16[8,1,6,512]{3,0,2,1:T(8,128)(2,1)S(1)}, bf16[8,1,6,512]{3,0,2,1:T(8,128)(2,1)S(1)}, u32[]{:S(2)}, u32[]{:S(2)}) collective-permute-start(bf16[8,1,6,512]{3,0,2,1:T(8,128)(2,1)S(1)} %get-tuple-element.114), channel_id=1, source_target_pairs={{1,0},{2,1},{3,2},{4,3},{5,4},{6,5},{7,6},{8,7},{9,8},{10,9},{11,1... | collective-permute-start | bytes 147464 | tf_op jit(solution)/shard_map/ppermute | solution.py:30
  704.9 17.3 %copy-start.1 = (bf16[3,3,3,512,512]{3,4,2,1,0:T(8,128)(2,1)S(1)}, bf16[3,3,3,512,512]{3,4,2,1,0:T(8,128)(2,1)}, u32[]{:S(2)}) copy-start(bf16[3,3,3,512,512]{3,4,2,1,0:T(8,128)(2,1)} %all-gather.6.cloned.1.call-done) | copy-start | bytes 42467332
  722.4 4.1 copy-start.4
Sparse Core Ops, SparseCore 0:
  61.2 73.0 all-gather.9
  137.0 75.8 all-gather.7
  323.0 82.2 reduce-scatter.1
  407.0 297.8 all-gather.5
where the time goes:
time: 742 us; the launch traced here: 734 us
  waiting for transfers between devices  494 us (67%)
  matrix products  122 us (16%)
  blocking collectives  48.6 us (7%)
  starting transfers between devices  28.9 us (4%)
  other arithmetic  16.8 us (2%)
  between operations  13.9 us (2%)
  local copies, waits for them, and re-layouts  8.45 us (1%)
    all_gather x1, waiting for transfers between devices, shards(): lax.all_gather(conv_weight, 'head', axis=4, tiled=True)  245 us
    reduce_scatter x1, waiting for transfers between devices, shards(): lax.psum_scatter(jnp.dot(flat_rows, out_weight, preferred_element_type=jn...  81.8 us
    all_gather x1, waiting for transfers between devices, shards(): key_rows = lax.all_gather(mixed[:, 1, 0], 'blk', axis=0, tiled=True)  78.6 us
    all_gather x1, waiting for transfers between devices, shards(): value_rows = lax.all_gather(mixed[:, 2, 0], 'blk', axis=0, tiled=True)  71.5 us
    all_to_all x1, blocking collectives, shards(): lax.all_to_all(sectioned, 'head', split_axis=2, concat_axis=0, tiled=True)  48.6 us
    dot_general x32, matrix products, absorb_block(): jnp.einsum('hqk,khd->hqd', weights.astype(jnp.bfloat16), value_block, pre...  47.4 us
    dot_general x32, matrix products, absorb_block(): jnp.einsum('qhd,khd->hqk', queries, key_block, preferred_element_type=jnp...  44.8 us
    dot_general x54, matrix products, convolve(): jnp.einsum('thwc,co->thwo', window, weight[tap_time, tap_row, tap_col], p...  26.1 us
  transfers between devices with their start and end apart: 12, of which 10 were waited for; matrix products, arithmetic and copies ran while one was open for 1% of the time, Pallas kernels for 0%

commit v1 on v0

v1 whole, which is shorter than its diff:
```python
import functools
import math

import jax
import jax.numpy as jnp
from jax import lax
from jax.experimental import pallas as pl
from jax.experimental.pallas import tpu as pltpu
from jax.sharding import PartitionSpec as P

HEADS = 16
HD = 128
D = 3072
QBLK = 128
QROWS = 512
CH = 512
NORM_EPS = 1e-06
BF = jnp.bfloat16
F32 = jnp.float32
COEF = math.log2(math.e) / math.sqrt(HD)
VMEM = 56 * 2**20

N = 16
GROUPS_XY = [[c + 2 * k for k in range(8)] for c in range(2)]
GROUPS_Z = [[x + 2 * k for k in range(8)] for x in range(2)]
CORE_SWAP = [(i, i ^ 1) for i in range(N)]


def ones_call(body, out_shape, scratch=(), name=None):
    return pl.pallas_call(
        body,
        out_shape=out_shape,
        scratch_shapes=scratch,
        compiler_params=pltpu.CompilerParams(vmem_limit_bytes=VMEM),
        name=name,
    )


def attention_body(sub, q_ref, own_ref, other_ref, o_ref, keys, vals):
    half = own_ref.shape[0]

    @pl.when(pl.program_id(0) == 0)
    def _():
        for s, ref in enumerate((own_ref, other_ref)):
            rows = pl.ds(s * half, half)
            keys[rows, :HD] = ref[:, :HD]
            keys[rows, HD:] = ref[:, :HD]
            vals[rows, :HD] = ref[:, HD:]
            vals[rows, HD:] = jnp.ones((half, HD), BF)

    def scores(i):
        q = q_ref[0, pl.ds(i * sub, sub), :].astype(F32) * COEF
        hi = q.astype(BF)
        lo = (q - hi.astype(F32)).astype(BF)
        return lax.dot_general(
            jnp.concatenate([hi, lo], axis=1),
            keys[...],
            (((1,), (1,)), ((), ())),
            preferred_element_type=F32,
        )

    lse_rows = []
    current = scores(0)
    for i in range(QROWS // sub):
        later = scores(i + 1) if (i + 1) * sub < QROWS else None
        high = jnp.max(current, axis=1, keepdims=True)
        weights = jnp.exp2(current - high).astype(BF)
        acc = jnp.dot(weights, vals[...], preferred_element_type=F32)
        total = acc[:, HD:]
        o_ref[0, pl.ds(i * sub, sub), :] = (acc[:, :HD] / total).astype(BF)
        lse = high + jnp.log2(total)
        for k in range(sub // 128):
            lse_rows.append(jnp.transpose(lse[k * 128 : (k + 1) * 128])[:1])
        current = later
    lse = jnp.concatenate(lse_rows, axis=0)
    hi = lse.astype(BF).astype(F32)
    mid = (lse - hi).astype(BF).astype(F32)
    low = lse - hi - mid
    tail = jnp.concatenate([hi, mid, low, jnp.zeros_like(hi)], axis=0)
    o_ref[0, QROWS:, :] = tail.astype(BF)


def attention(queries, own, other):
    chunks = queries.shape[0]
    half = own.shape[0]
    whole = pl.BlockSpec((half, 2 * HD), lambda i: (0, 0))
    return pl.pallas_call(
        functools.partial(attention_body, 256),
        grid=(chunks,),
        in_specs=[pl.BlockSpec((1, QROWS, HD), lambda i: (i, 0, 0)), whole, whole],
        out_specs=pl.BlockSpec((1, QROWS + 16, HD), lambda i: (i, 0, 0)),
        out_shape=jax.ShapeDtypeStruct((chunks, QROWS + 16, HD), BF),
        scratch_shapes=[pltpu.VMEM((2 * half, 2 * HD), BF), pltpu.VMEM((2 * half, 2 * HD), BF)],
        compiler_params=pltpu.CompilerParams(vmem_limit_bytes=VMEM),
        name="attention",
    )(queries, own, other)


def merge_body(part_ref, o_ref):
    count = part_ref.shape[0]
    lses = []
    for s in range(count):
        tail = part_ref[s, QROWS:, :].astype(F32)
        lses.append(tail[0:4] + tail[4:8] + tail[8:12])
    high = functools.reduce(jnp.maximum, lses)
    shares = [jnp.exp2(v - high) for v in lses]
    total = functools.reduce(jnp.add, shares)
    shares = [v / total for v in shares]
    for k in range(4):
        acc = jnp.zeros((128, HD), F32)
        for s in range(count):
            column = jnp.transpose(jnp.broadcast_to(shares[s][k : k + 1], (128, 128)))
            acc = acc + column * part_ref[s, pl.ds(k * 128, 128), :].astype(F32)
        o_ref[pl.ds(k * 128, 128), :] = acc.astype(BF)


def merge(parts):
    return ones_call(merge_body, jax.ShapeDtypeStruct((QROWS, HD), BF), name="merge")(parts)


def patch_body(att_ref, wa_ref, wb_ref, scale_ref, shift_ref, fw_ref, fb_ref, o_ref, rows, x):
    step = pl.program_id(0)
    cols = wa_ref.shape[1]

    @pl.when(step == 0)
    def _():
        for h in range(HEADS):
            rows[:, h * HD : (h + 1) * HD] = att_ref[h]

    a = rows[...]
    x[0, step] = jnp.dot(a, wa_ref[...], preferred_element_type=F32)
    x[1, step] = jnp.dot(a, wb_ref[...], preferred_element_type=F32)

    @pl.when(step == pl.num_programs(0) - 1)
    def _():
        steps = x.shape[1]
        parts = [x[s, i] for s in range(2) for i in range(steps)]
        mean = sum(jnp.sum(p, axis=1, keepdims=True) for p in parts) * (1.0 / D)
        parts = [p - mean for p in parts]
        var = sum(jnp.sum(p * p, axis=1, keepdims=True) for p in parts) * (1.0 / D)
        rstd = lax.rsqrt(var + NORM_EPS)
        acc = jnp.zeros(o_ref.shape, F32)
        for n, p in enumerate(parts):
            span = pl.ds(n * cols, cols)
            m = (p * rstd * (1.0 + scale_ref[:, span]) + shift_ref[:, span]).astype(BF)
            acc = acc + jnp.dot(m, fw_ref[span, :], preferred_element_type=F32)
        o_ref[...] = (acc + fb_ref[...]).astype(BF)


def patch_rows(att, wa, wb, scale, shift, fw, fb):
    half = wa.shape[1]
    cols = 512
    steps = half // cols
    block = pl.BlockSpec((HEADS * HD, cols), lambda i: (0, i))

    def whole(arr):
        return pl.BlockSpec(arr.shape, lambda i: (0,) * arr.ndim)

    count = att.shape[1]
    return pl.pallas_call(
        patch_body,
        grid=(steps,),
        in_specs=[whole(att), block, block, whole(scale), whole(shift), whole(fw), whole(fb)],
        out_specs=pl.BlockSpec((count, fw.shape[1]), lambda i: (0, 0)),
        out_shape=jax.ShapeDtypeStruct((count, fw.shape[1]), BF),
        scratch_shapes=[
            pltpu.VMEM((count, HEADS * HD), BF),
            pltpu.VMEM((2, steps, count, cols), F32),
        ],
        compiler_params=pltpu.CompilerParams(vmem_limit_bytes=VMEM),
        name="patches",
    )(att, wa, wb, scale, shift, fw, fb)


def conv_body(e_ref, w1_ref, b1_ref, mask_ref, w2_ref, b2_ref, o_ref, feat):
    wide = 512
    for j in range(2):
        lhs = jnp.concatenate([e_ref[j, a : a + 8] for a in range(3)], axis=-1)
        lhs = lhs.reshape(8 * 3 * 16, lhs.shape[-1])
        for n in range(2048 // wide):
            span = pl.ds(n * wide, wide)
            v = jnp.dot(lhs, w1_ref[:, span], preferred_element_type=F32) + b1_ref[:, span]
            v = v / (1.0 + jnp.exp(-v))
            v = v.reshape(8, 3, 16, wide) * mask_ref[:, :, span][None]
            v = v.astype(BF)
            feat[j, 2:, :, :, span] = v
            feat[j, 0, :, :, span] = v[0]
            feat[j, 1, :, :, span] = v[0]
    lane = lax.broadcasted_iota(jnp.int32, (128, 128), 1)
    col = lax.broadcasted_iota(jnp.int32, (128, 128), 0) % 16
    for y in range(4):
        acc = jnp.zeros((256, 128), F32)
        for a in range(3):
            for b in range(3):
                r, ey = divmod(y + b, 2)
                lhs = feat[:, a : a + 8, r, :, pl.ds(ey * 1024, 1024)].reshape(256, 1024)
                acc = acc + jnp.dot(lhs, w2_ref[a * 3 + b], preferred_element_type=F32)
        z0, z1 = acc[:128], acc[128:]
        right = jnp.where(col == 0, 0.0, pltpu.roll(z1, 1, 0))
        left = jnp.where(col == 15, 0.0, pltpu.roll(z0, 127, 0))
        s0 = z0 + pltpu.roll(jnp.where(lane < 96, right, z1), 64, 1)
        s1 = z1 + pltpu.roll(jnp.where(lane < 96, z0, left), 64, 1)
        out = jnp.where(lane < 64, s0, pltpu.roll(s1, 64, 1)) + b2_ref[...]
        o_ref[y] = out.astype(BF).reshape(8, 16, 128)


def conv_stage(e, w1, b1, mask, w2, b2):
    return ones_call(
        conv_body,
        jax.ShapeDtypeStruct((4, 8, 16, 128), BF),
        [pltpu.VMEM((2, 10, 3, 16, 2048), BF)],
        name="convs",
    )(e, w1, b1, mask, w2, b2)


def first_weights(k):
    outs = []
    for ey in range(2):
        for ex in range(2):
            wide = jnp.pad(k, ((0, 0), (ey, 1 - ey), (ex + 1, 2 - ex), (0, 0), (0, 0)))
            wide = wide.reshape(3, 2, 2, 3, 2, 16, CH)
            outs.append(jnp.transpose(wide, (0, 1, 3, 5, 2, 4, 6)).reshape(3 * 2 * 3 * 64, CH))
    return jnp.concatenate(outs, axis=1)


def second_weights(k):
    g = [k[:, :, i] for i in range(3)]
    none = jnp.zeros_like(g[0])
    even = jnp.concatenate([g[1], g[0], none, g[2]], axis=-1)
    odd = jnp.concatenate([g[2], g[1], g[0], none], axis=-1)
    return jnp.concatenate([even, odd], axis=2).reshape(9, 2 * CH, 128)


def window(rows):
    field = jnp.transpose(rows, (1, 2, 0, 3))
    zero = jnp.zeros_like(field[:, :, :1, :64])
    before = jnp.concatenate([zero, field[:, :, :-1, 64:]], axis=2)
    after = jnp.concatenate([field[:, :, 1:, :64], zero], axis=2)
    both = jnp.stack(
        [jnp.concatenate([before, field], axis=-1), jnp.concatenate([field, after], axis=-1)]
    )
    pairs = jnp.concatenate([both[:, :, :3], both[:, :, 1:]], axis=-1)
    return jnp.concatenate([pairs[:, :1], pairs[:, :1], pairs], axis=1)


def shards(
    qkv,
    query_blocks,
    out_weight,
    mod_shift,
    mod_scale,
    final_weight,
    final_bias,
    conv_in_weight,
    conv_in_bias,
    conv_weight,
    conv_bias,
):
    head = lax.axis_index("head")
    blk = lax.axis_index("blk")
    core = blk % 2
    tok = qkv.shape[1]

    parts = qkv.reshape(tok, 3, HEADS, HD)
    q_send = jnp.transpose(parts[:, 0], (1, 0, 2))
    kv_send = jnp.concatenate([parts[:, 1], parts[:, 2]], axis=-1)
    kv_send = jnp.transpose(kv_send, (1, 0, 2))
    q_all = lax.all_to_all(q_send, "head", 0, 0, tiled=True)
    kv_own = lax.all_to_all(kv_send, "head", 0, 0, tiled=True).reshape(-1, 2 * HD)

    half = lax.dynamic_slice_in_dim(out_weight, core * (D // 2), D // 2, axis=1)
    paired = lax.ppermute(half, "head", CORE_SWAP)
    even = (head % 2) == 0
    pair = jnp.stack([jnp.where(even, half, paired), jnp.where(even, paired, half)])
    weight_a = lax.all_gather(pair, "head", axis=0, tiled=True, axis_index_groups=GROUPS_Z)
    weight_a = weight_a.reshape(HEADS * HD, D // 2)
    weight_b = lax.ppermute(weight_a, "blk", CORE_SWAP)

    chosen = query_blocks % N
    queries = jnp.take(q_all.reshape(N, QBLK, HD), chosen, axis=0).reshape(1, QROWS, HD)
    queries = lax.all_to_all(
        jnp.broadcast_to(queries, (8, QROWS, HD)),
        "blk",
        0,
        0,
        tiled=True,
        axis_index_groups=GROUPS_XY,
    )
    kv_other = lax.ppermute(kv_own, "blk", CORE_SWAP)
    partial = attention(queries, kv_own, kv_other)
    partial = lax.all_to_all(partial, "blk", 0, 0, tiled=True, axis_index_groups=GROUPS_XY)
    attended = merge(partial).reshape(N, QROWS // N, HD)
    attended = lax.all_to_all(attended, "head", 0, 0, tiled=True)

    def own_first(arr, axis):
        return jnp.where(core == 0, arr, jnp.roll(arr, D // 2, axis=axis))

    patches = patch_rows(
        attended,
        weight_a,
        weight_b,
        own_first(mod_scale.reshape(1, D), 1),
        own_first(mod_shift.reshape(1, D), 1),
        own_first(final_weight, 0),
        final_bias.reshape(1, -1),
    )

    tile = patches.reshape(8, 2, 128)
    ends = N - 1
    above = lax.ppermute(tile[:, 1:], "blk", [(i, i + 1) for i in range(ends)])
    below = lax.ppermute(tile[:, :1], "blk", [(i + 1, i) for i in range(ends)])
    rows = jnp.concatenate([above, tile, below], axis=1)
    rows = lax.all_to_all(
        jnp.broadcast_to(rows[None], (N,) + rows.shape), "head", 0, 0, tiled=True
    )

    inside = jnp.ones((3, 2, 2 * CH), F32)
    inside = inside.at[0, 0].set(jnp.where(blk == 0, 0.0, 1.0))
    inside = inside.at[2, 1].set(jnp.where(blk == N - 1, 0.0, 1.0))
    bias_out = lax.dynamic_slice_in_dim(conv_bias, head * 32, 32)
    out = conv_stage(
        window(rows),
        first_weights(conv_in_weight),
        jnp.tile(conv_in_bias, 4).reshape(1, -1),
        inside.reshape(3, 1, 4 * CH),
        second_weights(conv_weight),
        jnp.tile(bias_out, 4).reshape(1, -1),
    )
    out = lax.all_to_all(jnp.transpose(out, (2, 0, 1, 3)), "head", 0, 0, tiled=True)
    out = jnp.transpose(out.reshape(N, 4, 8, 4, 32), (2, 1, 3, 0, 4))
    return out.reshape(8, 4, 4, CH)


def solution(mesh):
    in_specs = (
        P("blk", "head", None),
        P("blk"),
        P("head", None),
        P(),
        P(),
        P(),
        P(),
        P(),
        P(),
        P(None, None, None, None, "head"),
        P(),
    )
    out_specs = P(None, "blk", "head", None)
    return jax.shard_map(shards, mesh=mesh, in_specs=in_specs, out_specs=out_specs, check_vma=False)
```

time: 742 us -> 325 us (0.44)
  waiting for transfers between devices: 494 us -> 142 us
  matrix products: 122 us -> 0 us
  Pallas kernels: 0 us -> 47.9 us
  local copies, waits for them, and re-layouts: 8.45 us -> 51.4 us
  blocking collectives: 48.6 us -> 14.1 us
  starting transfers between devices: 28.9 us -> 39.4 us
    all_gather x3 -> x1, waiting for transfers between devices: 395 us -> 77.6 us  [shards(): lax.all_gather(pair, 'head', axis=0, tiled=True, axis_index_groups=GROUPS_Z)]
    dot_general x120 -> x0, matrix products: 122 us -> none  [the longest x32 47.4 us: absorb_block(): jnp.einsum('hqk,khd->hqd', weights.astype(jnp.bfloat16), value_block, pre...]
    reduce_scatter x1 -> x0, waiting for transfers between devices: 81.8 us -> none  [shards(): lax.psum_scatter(jnp.dot(flat_rows, out_weight, preferred_element_type=jn...]
    all_to_all x0 -> x6, waiting for transfers between devices: none -> 49.8 us  [the longest x1 17.5 us: shards(): q_all = lax.all_to_all(q_send, 'head', 0, 0, tiled=True)]
    pallas_call x0 -> x4, Pallas kernels: none -> 47.9 us  [the longest x1 23.9 us: attention(): pl.pallas_call(functools.partial(attention_body, 256), grid=(chunks,), in...]
    all_to_all x1, blocking collectives: 48.6 us -> 14.1 us  [shards(): lax.all_to_all(jnp.transpose(out, (2, 0, 1, 3)), 'head', 0, 0, tiled=True)]
    all_to_all x0 -> x6, starting transfers between devices: none -> 33.8 us  [the longest x1 7.8 us: shards(): attended = lax.all_to_all(attended, 'head', 0, 0, tiled=True)]
    reshape x2 -> x12, local copies, waits for them, and re-layouts: 2.5 us -> 27.7 us  [the longest x4 13.4 us: first_weights(): jnp.transpose(wide, (0, 1, 3, 5, 2, 4, 6)).reshape(3 * 2 * 3 * 64, CH)]
  transfers between devices with their start and end apart: 12 -> 12, of which waited for: 10 -> 8; matrix products, arithmetic and copies ran while one was open for 1% -> 18% of each run, Pallas kernels for 0% -> 8%
where the time goes in v1:
time: 325 us; the launch traced here: 324 us
  waiting for transfers between devices  142 us (44%)
  local copies, waits for them, and re-layouts  51.4 us (16%)
  Pallas kernels  47.9 us (15%)
  starting transfers between devices  39.4 us (12%)
  other arithmetic  15.4 us (5%)
  blocking collectives  14.1 us (4%)
  between operations  13.7 us (4%)
    all_gather x1, waiting for transfers between devices, shards(): lax.all_gather(pair, 'head', axis=0, tiled=True, axis_index_groups=GROUPS_Z)  77.6 us
    pallas_call x1, Pallas kernels, attention(): pl.pallas_call(functools.partial(attention_body, 256), grid=(chunks,), in...  23.9 us
    all_to_all x1, waiting for transfers between devices, shards(): q_all = lax.all_to_all(q_send, 'head', 0, 0, tiled=True)  17.5 us
    all_to_all x1, blocking collectives, shards(): lax.all_to_all(jnp.transpose(out, (2, 0, 1, 3)), 'head', 0, 0, tiled=True)  14.1 us
    pallas_call x1, Pallas kernels, conv_stage(): ones_call(conv_body, jax.ShapeDtypeStruct((4, 8, 16, 128), BF), [pltpu.VM...  14 us
    reshape x4, local copies, waits for them, and re-layouts, first_weights(): jnp.transpose(wide, (0, 1, 3, 5, 2, 4, 6)).reshape(3 * 2 * 3 * 64, CH)  13.4 us
    reshape x4, local copies, waits for them, and re-layouts, first_weights(): wide = wide.reshape(3, 2, 2, 3, 2, 16, CH)  11.5 us
    all_to_all x1, waiting for transfers between devices, shards(): lax.all_to_all(jnp.broadcast_to(queries, (8, QROWS, HD)), 'blk', 0, 0, ti...  10.9 us
  transfers between devices with their start and end apart: 12, of which 8 were waited for; matrix products, arithmetic and copies ran while one was open for 18% of the time, Pallas kernels for 8%

profile of v1, /device:TPU:4, one launch (start us, length us, event | category | flops | bytes accessed | tf_op | source)
XLA Modules:
  0.0 323.7 jit_solution(5858109724038553946)
XLA Ops:
  9.0 9.7 %collective-permute-done.1 = bf16[128,1536]{1,0:T(8,128)(2,1)S(1)} collective-permute-done((bf16[128,1536]{1,0:T(8,128)(2,1)S(1)}, bf16[128,1536]{1,0:T(8,128)(2,1)S(1)}, u32[]{:S(2)}, u32[]{:S(2)}) %collective-permute-start.1) | collective-permute-done | bytes 393248 | tf_op jit(solution)/shard_map/ppermute | solution.py:272
  20.8 77.6 %all-gather.2.cloned.1.call-done = bf16[16,128,1536]{2,1,0:T(8,128)(2,1)} async-done(((bf16[2,128,1536]{2,1,0:T(8,128)(2,1)}), bf16[16,128,1536]{2,1,0:T(8,128)(2,1)}) %all-gather.2.cloned.1.call-update) | async-done | bytes 6291472 | tf_op jit(solution)/shard_map/all_gather | solution.py:275
  100.5 5.0 %all-to-all-start = ((bf16[16,128,128]{2,1,0:T(8,128)(2,1)}), bf16[16,128,128]{2,1,0:T(8,128)(2,1)S(1)}, u32[]{:S(2)}, u32[]{:S(2)}) async-start(bf16[16,128,128]{2,1,0:T(8,128)(2,1)} %bitcast.3), calls=%async_computation | async-start | bytes 1048576 | tf_op jit(solution)/shard_map/all_to_all | solution.py:268
  106.6 17.5 %all-to-all-done = bf16[16,128,128]{2,1,0:T(8,128)(2,1)S(1)} async-done(((bf16[16,128,128]{2,1,0:T(8,128)(2,1)}), bf16[16,128,128]{2,1,0:T(8,128)(2,1)S(1)}, u32[]{:S(2)}, u32[]{:S(2)}) %all-to-all-start) | async-done | bytes 524320 | tf_op jit(solution)/shard_map/all_to_all | solution.py:268
  124.1 4.5 %all-to-all-start.2 = ((bf16[16,128,256]{1,2,0:T(8,128)(2,1)}), bf16[16,128,256]{1,2,0:T(8,128)(2,1)}, u32[]{:S(2)}, u32[]{:S(2)}) async-start(bf16[16,128,256]{1,2,0:T(8,128)(2,1)} %maximum_bitcast_fusion), calls=%async_computation.2 | async-start | bytes 2097152 | tf_op jit(solution)/shard_map/all_to_all | solution.py:269
  133.3 3.0 reshape.164
  136.3 2.2 copy.77
  138.5 3.0 reshape.162
  141.5 3.5 %copy.78 = bf16[3,2,2,3,2,16,512]{6,4,2,5,3,1,0:T(2,128)(2,1)} copy(bf16[3,2,2,3,2,16,512]{6,5,4,3,2,1,0:T(8,128)(2,1)} %bitcast.76) | data formatting | bytes 2359296 | tf_op jit(solution)/shard_map/reshape | solution.py:221
  145.0 3.7 %reshape.160 = bf16[1152,512]{1,0:T(8,128)(2,1)} reshape(bf16[3,2,3,16,2,2,512]{6,5,4,3,2,1,0:T(2,128)(2,1)} %bitcast.81) | data formatting | bytes 2359296 | tf_op jit(solution)/shard_map/reshape | solution.py:222
  148.7 3.5 %copy.79 = bf16[3,2,2,3,2,16,512]{6,4,2,5,3,1,0:T(2,128)(2,1)} copy(bf16[3,2,2,3,2,16,512]{6,5,4,3,2,1,0:T(8,128)(2,1)} %bitcast.75) | data formatting | bytes 2359296 | tf_op jit(solution)/shard_map/reshape | solution.py:221
  152.3 3.7 %reshape.158 = bf16[1152,512]{1,0:T(8,128)(2,1)} reshape(bf16[3,2,3,16,2,2,512]{6,5,4,3,2,1,0:T(2,128)(2,1)} %bitcast.82) | data formatting | bytes 2359296 | tf_op jit(solution)/shard_map/reshape | solution.py:222
  157.4 2.3 gather_fusion
  159.7 2.3 copy.53
  164.2 7.3 %all-to-all-start.1 = ((bf16[8,512,128]{2,1,0:T(8,128)(2,1)}), bf16[8,512,128]{2,1,0:T(8,128)(2,1)}, u32[]{:S(2)}, u32[]{:S(2)}) async-start(bf16[8,512,128]{2,1,0:T(8,128)(2,1)} %broadcast_in_dim.39), calls=%async_computation.1 | async-start | bytes 2097152 | tf_op jit(solution)/shard_map/all_to_all | solution.py:281
  175.5 10.9 %all-to-all-done.1.q_ref = bf16[8,512,128]{2,1,0:T(8,128)(2,1)} async-done(((bf16[8,512,128]{2,1,0:T(8,128)(2,1)}), bf16[8,512,128]{2,1,0:T(8,128)(2,1)}, u32[]{:S(2)}, u32[]{:S(2)}) %all-to-all-start.1) | async-done | bytes 1048608 | tf_op jit(solution)/shard_map/all_to_all | solution.py:281
  186.4 23.9 %attention.1 = bf16[8,528,128]{2,1,0:T(8,128)(2,1)} custom-call(bf16[8,512,128]{2,1,0:T(8,128)(2,1)} %all-to-all-done.1.q_ref, bf16[2048,256]{1,0:T(8,128)(2,1)} %bitcast.84, bf16[2048,256]{1,0:T(8,128)(2,1)} %collective-permute-done.other_ref), custom_call_target="tpu_custom_call" | custom-call | tf_op jit(solution)/shard_map/attention/pallas_call | solution.py:87
  210.3 5.7 %all-to-all-start.3 = ((bf16[8,528,128]{2,1,0:T(8,128)(2,1)}), bf16[8,528,128]{2,1,0:T(8,128)(2,1)}, u32[]{:S(2)}, u32[]{:S(2)}) async-start(bf16[8,528,128]{2,1,0:T(8,128)(2,1)} %attention.1), calls=%async_computation.3 | async-start | bytes 2162688 | tf_op jit(solution)/shard_map/all_to_all | solution.py:291
  217.4 3.8 %pad_maximum_fusion.w1_ref = bf16[1152,2048]{1,0:T(8,128)(2,1)} fusion(bf16[1152,512]{1,0:T(8,128)(2,1)S(1)} %reshape.164, bf16[1152,512]{1,0:T(8,128)(2,1)S(1)} %reshape.162, bf16[1152,512]{1,0:T(8,128)(2,1)S(1)} %copy-done.1, bf16[1152,512]{1,0:T(8,128)(2,1)} %reshape.158), kind=kLoop, calls=%fused_computation.1 | loop fusion | flops 18874368 | bytes 9437184 | tf_op jit(solution)/shard_map/concatenate | solution.py:223
  221.2 9.7 %all-to-all-done.3.part_ref = bf16[8,528,128]{2,1,0:T(8,128)(2,1)} async-done(((bf16[8,528,128]{2,1,0:T(8,128)(2,1)}), bf16[8,528,128]{2,1,0:T(8,128)(2,1)}, u32[]{:S(2)}, u32[]{:S(2)}) %all-to-all-start.3) | async-done | bytes 1081376 | tf_op jit(solution)/shard_map/all_to_all | solution.py:291
  230.9 2.5 merge.1
  233.5 7.8 %all-to-all-start.4 = ((bf16[16,32,128]{2,1,0:T(8,128)(2,1)}), bf16[16,32,128]{2,1,0:T(8,128)(2,1)S(1)}, u32[]{:S(2)}, u32[]{:S(2)}) async-start(bf16[16,32,128]{2,1,0:T(8,128)(2,1)} %bitcast.89), calls=%async_computation.4 | async-start | bytes 262144 | tf_op jit(solution)/shard_map/all_to_all | solution.py:293
  242.5 8.4 %all-to-all-done.4.att_ref = bf16[16,32,128]{2,1,0:T(8,128)(2,1)S(1)} async-done(((bf16[16,32,128]{2,1,0:T(8,128)(2,1)}), bf16[16,32,128]{2,1,0:T(8,128)(2,1)S(1)}, u32[]{:S(2)}, u32[]{:S(2)}) %all-to-all-start.4) | async-done | bytes 131104 | tf_op jit(solution)/shard_map/all_to_all | solution.py:293
  251.5 7.5 %patches.1 = bf16[32,64]{1,0:T(8,128)(2,1)} custom-call(bf16[16,32,128]{2,1,0:T(8,128)(2,1)} %copy-done.4, bf16[2048,1536]{1,0:T(8,128)(2,1)} %bitcast.74, bf16[2048,1536]{1,0:T(8,128)(2,1)} %collective-permute-done.2.wb_ref, f32[1,3072]{1,0:T(1,128)} %bitcast.92, f32[1,3072]{1,0:T(1,128)} %bitcast.93, bf16[3072,64]{1,0:T(8,128)(2,1)} %maximum_select_fusion.fw_ref, ...), custom_call_target="tpu_custom_call" | custom-call | tf_op jit(solution)/shard_map/patches/pallas_call | solution.py:160
  261.8 2.4 collective-permute-start.3
  265.6 4.7 %collective-permute-done.3 = bf16[8,1,128]{2,1,0:T(2,128)(2,1)S(1)} collective-permute-done((bf16[8,1,128]{2,1,0:T(2,128)(2,1)S(1)}, bf16[8,1,128]{2,1,0:T(2,128)(2,1)S(1)}, u32[]{:S(2)}, u32[]{:S(2)}) %collective-permute-start.3) | collective-permute-done | bytes 2080 | tf_op jit(solution)/shard_map/ppermute | solution.py:310
  271.0 3.5 %all-to-all-start.5 = ((bf16[16,8,4,128]{3,2,1,0:T(4,128)(2,1)}), bf16[16,8,4,128]{3,2,1,0:T(4,128)(2,1)S(1)}, u32[]{:S(2)}, u32[]{:S(2)}) async-start(bf16[16,8,4,128]{3,2,1,0:T(4,128)(2,1)} %broadcast_in_dim.40), calls=%async_computation.5 | async-start | bytes 262144 | tf_op jit(solution)/shard_map/all_to_all | solution.py:313
  274.6 2.3 maximum_maximum_fusion
  276.9 2.5 copy.64
  280.9 3.4 %all-to-all-done.5 = bf16[16,8,4,128]{3,2,1,0:T(4,128)(2,1)S(1)} async-done(((bf16[16,8,4,128]{3,2,1,0:T(4,128)(2,1)}), bf16[16,8,4,128]{3,2,1,0:T(4,128)(2,1)S(1)}, u32[]{:S(2)}, u32[]{:S(2)}) %all-to-all-start.5) | async-done | bytes 131104 | tf_op jit(solution)/shard_map/all_to_all | solution.py:313
  285.9 14.0 %convs.1 = bf16[4,8,16,128]{3,2,1,0:T(8,128)(2,1)} custom-call(bf16[2,10,3,16,384]{4,3,2,1,0:T(8,128)(2,1)} %maximum_maximum_fusion.1.e_ref, bf16[1152,2048]{1,0:T(8,128)(2,1)} %pad_maximum_fusion.w1_ref, f32[1,2048]{1,0:T(1,128)} %bitcast.94, f32[3,1,2048]{2,1,0:T(1,128)} %reshape.166.mask_ref, bf16[9,1024,128]{2,1,0:T(8,128)(2,1)} %bitcast.71, ...), custom_call_target="tpu_custom_call" | custom-call | tf_op jit(solution)/shard_map/convs/pallas_call | solution.py:208
  300.8 14.1 %all_to_all.35 = bf16[16,4,8,128]{3,2,1,0:T(8,128)(2,1)S(1)} all-to-all(bf16[16,4,8,128]{3,2,1,0:T(8,128)(2,1)S(1)} %copy.65), channel_id=1, replica_groups=mesh['head'=16,'blk'=16] {'head'}, dimensions={0} | all-to-all | bytes 262144 | tf_op jit(solution)/shard_map/all_to_all | solution.py:329
  (74 shorter events, 34.1 us)
Async XLA Ops:
  6.5 257.7 %copy-start = (f32[512]{0:T(512)S(1)}, f32[512]{0:T(512)}, u32[]{:S(2)}) copy-start(f32[512]{0:T(512)} %param.23) | copy-start | bytes 6148
  6.5 91.8 %all-gather.2.cloned.1.call-start = ((), (), s32[]{:S(2)}) async-start(), calls=%async_computation.7 | async-start | bytes 7077888 | tf_op jit(solution)/shard_map/all_gather | solution.py:275
  6.5 91.8 %copy-start.2 = (bf16[1,128,6144]{2,1,0:T(8,128)(2,1)S(1)}, bf16[1,128,6144]{2,1,0:T(8,128)(2,1)}, u32[]{:S(2)}) copy-start(bf16[1,128,6144]{2,1,0:T(8,128)(2,1)} %param.15) | copy-start | bytes 4718596
  7.7 10.9 %collective-permute-start.1 = (bf16[128,1536]{1,0:T(8,128)(2,1)S(1)}, bf16[128,1536]{1,0:T(8,128)(2,1)S(1)}, u32[]{:S(2)}, u32[]{:S(2)}) collective-permute-start(bf16[128,1536]{1,0:T(8,128)(2,1)S(1)} %constant_dynamic-slice_fusion), channel_id=1, source_target_pairs={{0,16},{16,0},{32,48},{48,32},{64,80},{80,64},{96,112},{112,96},{1... | collective-permute-start | bytes 1179656 | tf_op jit(solution)/shard_map/ppermute | solution.py:272
  98.3 152.6 %collective-permute-start.2 = (bf16[2048,1536]{1,0:T(8,128)(2,1)}, bf16[2048,1536]{1,0:T(8,128)(2,1)}, u32[]{:S(2)}, u32[]{:S(2)}) collective-permute-start(bf16[2048,1536]{1,0:T(8,128)(2,1)} %bitcast.73), channel_id=1, source_target_pairs={{0,1},{1,0},{2,3},{3,2},{4,5},{5,4},{6,7},{7,6},{8,9},{9,8},{10,11... | collective-permute-start | bytes 18874376 | tf_op jit(solution)/shard_map/ppermute | solution.py:277
  100.5 23.6 %all-to-all-start = ((bf16[16,128,128]{2,1,0:T(8,128)(2,1)}), bf16[16,128,128]{2,1,0:T(8,128)(2,1)S(1)}, u32[]{:S(2)}, u32[]{:S(2)}) async-start(bf16[16,128,128]{2,1,0:T(8,128)(2,1)} %bitcast.3), calls=%async_computation | async-start | bytes 1048576 | tf_op jit(solution)/shard_map/all_to_all | solution.py:268
  105.5 23.1 %copy-start.6 = (bf16[3072,64]{0,1:T(8,128)(2,1)S(1)}, bf16[3072,64]{0,1:T(8,128)(2,1)}, u32[]{:S(2)}) copy-start(bf16[3072,64]{0,1:T(8,128)(2,1)} %param.20) | copy-start | bytes 1179652
  105.6 23.5 %copy-start.5 = (bf16[3,3,3,16,512]{4,3,2,1,0:T(8,128)(2,1)S(1)}, bf16[3,3,3,16,512]{4,3,2,1,0:T(8,128)(2,1)}, u32[]{:S(2)}) copy-start(bf16[3,3,3,16,512]{4,3,2,1,0:T(8,128)(2,1)} %param.22) | copy-start | bytes 1327108
  124.1 7.0 %copy-start.3 = (bf16[16,128,128]{2,1,0:T(8,128)(2,1)}, bf16[16,128,128]{2,1,0:T(8,128)(2,1)S(1)}, u32[]{:S(2)}) copy-start(bf16[16,128,128]{2,1,0:T(8,128)(2,1)S(1)} %all-to-all-done) | copy-start | bytes 1572868
  124.1 35.6 %all-to-all-start.2 = ((bf16[16,128,256]{1,2,0:T(8,128)(2,1)}), bf16[16,128,256]{1,2,0:T(8,128)(2,1)}, u32[]{:S(2)}, u32[]{:S(2)}) async-start(bf16[16,128,256]{1,2,0:T(8,128)(2,1)} %maximum_bitcast_fusion), calls=%async_computation.2 | async-start | bytes 2097152 | tf_op jit(solution)/shard_map/all_to_all | solution.py:269
  148.7 7.3 %copy-start.8 = (s32[4]{0:T(128)S(1)}, s32[4]{0:T(128)}, u32[]{:S(2)}) copy-start(s32[4]{0:T(128)} %param.16) | copy-start | bytes 52
  159.7 11.7 %copy-start.7 = (f32[3072]{0:T(1024)S(1)}, f32[3072]{0:T(1024)}, u32[]{:S(2)}) copy-start(f32[3072]{0:T(1024)} %param.19) | copy-start | bytes 36868
  162.0 24.5 %collective-permute-start = (bf16[2048,256]{1,0:T(8,128)(2,1)}, bf16[2048,256]{1,0:T(8,128)(2,1)}, u32[]{:S(2)}, u32[]{:S(2)}) collective-permute-start(bf16[2048,256]{1,0:T(8,128)(2,1)} %bitcast.83), channel_id=1, source_target_pairs={{0,1},{1,0},{2,3},{3,2},{4,5},{5,4},{6,7},{7,6},{8,9},{9,8},{10,11... | collective-permute-start | bytes 3145736 | tf_op jit(solution)/shard_map/ppermute | solution.py:289
  164.2 22.3 %all-to-all-start.1 = ((bf16[8,512,128]{2,1,0:T(8,128)(2,1)}), bf16[8,512,128]{2,1,0:T(8,128)(2,1)}, u32[]{:S(2)}, u32[]{:S(2)}) async-start(bf16[8,512,128]{2,1,0:T(8,128)(2,1)} %broadcast_in_dim.39), calls=%async_computation.1 | async-start | bytes 2097152 | tf_op jit(solution)/shard_map/all_to_all | solution.py:281
  175.5 41.9 %copy-start.1 = (bf16[1152,512]{1,0:T(8,128)(2,1)S(1)}, bf16[1152,512]{1,0:T(8,128)(2,1)}, u32[]{:S(2)}) copy-start(bf16[1152,512]{1,0:T(8,128)(2,1)} %reshape.160) | copy-start | bytes 3538948
  210.3 20.6 %all-to-all-start.3 = ((bf16[8,528,128]{2,1,0:T(8,128)(2,1)}), bf16[8,528,128]{2,1,0:T(8,128)(2,1)}, u32[]{:S(2)}, u32[]{:S(2)}) async-start(bf16[8,528,128]{2,1,0:T(8,128)(2,1)} %attention.1), calls=%async_computation.3 | async-start | bytes 2162688 | tf_op jit(solution)/shard_map/all_to_all | solution.py:291
  233.5 17.4 %all-to-all-start.4 = ((bf16[16,32,128]{2,1,0:T(8,128)(2,1)}), bf16[16,32,128]{2,1,0:T(8,128)(2,1)S(1)}, u32[]{:S(2)}, u32[]{:S(2)}) async-start(bf16[16,32,128]{2,1,0:T(8,128)(2,1)} %bitcast.89), calls=%async_computation.4 | async-start | bytes 262144 | tf_op jit(solution)/shard_map/all_to_all | solution.py:293
  250.9 0.7 copy-start.4
  259.9 5.8 %collective-permute-start.4 = (bf16[8,1,128]{2,1,0:T(2,128)(2,1)S(1)}, bf16[8,1,128]{2,1,0:T(2,128)(2,1)S(1)}, u32[]{:S(2)}, u32[]{:S(2)}) collective-permute-start(bf16[8,1,128]{2,1,0:T(2,128)(2,1)S(1)} %get-tuple-element.56), channel_id=1, source_target_pairs={{1,0},{2,1},{3,2},{4,3},{5,4},{6,5},{7,6},{8,7},{9,8},{10,9},{11,1... | collective-permute-start | bytes 6152 | tf_op jit(solution)/shard_map/ppermute | solution.py:311
  261.8 8.5 %collective-permute-start.3 = (bf16[8,1,128]{2,1,0:T(2,128)(2,1)S(1)}, bf16[8,1,128]{2,1,0:T(2,128)(2,1)S(1)}, u32[]{:S(2)}, u32[]{:S(2)}) collective-permute-start(bf16[8,1,128]{2,1,0:T(2,128)(2,1)S(1)} %get-tuple-element.55), channel_id=1, source_target_pairs={{0,1},{1,2},{2,3},{3,4},{4,5},{5,6},{6,7},{7,8},{8,9},{9,10},{10,1... | collective-permute-start | bytes 6152 | tf_op jit(solution)/shard_map/ppermute | solution.py:310
  271.0 13.2 %all-to-all-start.5 = ((bf16[16,8,4,128]{3,2,1,0:T(4,128)(2,1)}), bf16[16,8,4,128]{3,2,1,0:T(4,128)(2,1)S(1)}, u32[]{:S(2)}, u32[]{:S(2)}) async-start(bf16[16,8,4,128]{3,2,1,0:T(4,128)(2,1)} %broadcast_in_dim.40), calls=%async_computation.5 | async-start | bytes 262144 | tf_op jit(solution)/shard_map/all_to_all | solution.py:313
Sparse Core Ops, SparseCore 0:
  20.9 77.3 all-gather.1

commit v2 on v1

v2 whole, which is shorter than its diff:
```python
import functools
import math

import jax
import jax.numpy as jnp
from jax import lax
from jax.experimental import pallas as pl
from jax.experimental.pallas import tpu as pltpu
from jax.sharding import PartitionSpec as P

HEADS = 16
HD = 128
D = 3072
QBLK = 128
QROWS = 512
CH = 512
NORM_EPS = 1e-06
BF = jnp.bfloat16
F32 = jnp.float32
COEF = math.log2(math.e) / math.sqrt(HD)
MIB = 2**20

N = 16
GROUPS_Z = [[x + 2 * k for k in range(8)] for x in range(2)]
GROUPS_Y = [[x * 8 + c + 2 * k for k in range(4)] for x in range(2) for c in range(2)]
NEXT_SWAP = [(i, i ^ 1) for i in range(N)]
FAR_SWAP = [(i, i ^ 8) for i in range(N)]


def ones_call(body, out_shape, scratch=(), name=None):
    return pl.pallas_call(
        body,
        out_shape=out_shape,
        scratch_shapes=scratch,
        compiler_params=pltpu.CompilerParams(vmem_limit_bytes=32 * MIB),
        name=name,
    )


def split_body(x_ref, q_ref, kv_ref):
    for h in range(HEADS):
        q_ref[h] = x_ref[0, :, pl.ds(h * HD, HD)]
        for part in (1, 2):
            span = pl.ds((part * HEADS + h) * HD, HD)
            kv_ref[h, :, pl.ds((part - 1) * HD, HD)] = x_ref[0, :, span]


def split_heads(qkv):
    tok = qkv.shape[1]
    shapes = [jax.ShapeDtypeStruct((HEADS, tok, k * HD), BF) for k in (1, 2)]
    return ones_call(split_body, shapes, name="split")(qkv)


def select_body(chosen_ref, q_ref, o_ref):
    for i in range(QROWS // QBLK):
        o_ref[pl.ds(i * QBLK, QBLK), :] = q_ref[chosen_ref[i] % N]


def select_queries(chosen, q_all):
    return pl.pallas_call(
        select_body,
        in_specs=[
            pl.BlockSpec(memory_space=pltpu.SMEM),
            pl.BlockSpec(memory_space=pltpu.VMEM),
        ],
        out_shape=jax.ShapeDtypeStruct((QROWS, HD), BF),
        name="select",
    )(chosen, q_all)


def store_lse(o_ref, lse):
    hi = lse.astype(BF).astype(F32)
    mid = (lse - hi).astype(BF).astype(F32)
    low = lse - hi - mid
    tail = jnp.concatenate([hi, mid, low, jnp.zeros_like(hi)], axis=0)
    o_ref[0, QROWS:, :] = tail.astype(BF)


def load_lse(ref, s):
    tail = ref[s, QROWS:, :].astype(F32)
    return tail[0:4] + tail[4:8] + tail[8:12]


def column(row):
    return jnp.transpose(jnp.broadcast_to(row, (128, 128)))


def attention_body(sub, place_ref, *refs):
    q_refs, (own_ref, other_ref, o_ref, keys, vals, q_now) = refs[:4], refs[4:]
    half = own_ref.shape[0]
    for m, q_ref in enumerate(q_refs):

        @pl.when(pl.program_id(0) == m)
        def _(q_ref=q_ref):
            q_now[...] = q_ref[...]

    @pl.when(pl.program_id(0) == 0)
    def _():
        for s, ref in enumerate((own_ref, other_ref)):
            rows = pl.ds(s * half, half)
            keys[rows, :HD] = ref[:, :HD]
            keys[rows, HD:] = ref[:, :HD]
            vals[rows, :HD] = ref[:, HD:]
            vals[rows, HD:] = jnp.ones((half, HD), BF)

    def scores(i):
        q = q_now[pl.ds(i * sub, sub), :].astype(F32) * COEF
        hi = q.astype(BF)
        lo = (q - hi.astype(F32)).astype(BF)
        return lax.dot_general(
            jnp.concatenate([hi, lo], axis=1),
            keys[...],
            (((1,), (1,)), ((), ())),
            preferred_element_type=F32,
        )

    lse_rows = []
    current = scores(0)
    for i in range(QROWS // sub):
        later = scores(i + 1) if (i + 1) * sub < QROWS else None
        high = jnp.max(current, axis=1, keepdims=True)
        weights = jnp.exp2(current - high).astype(BF)
        acc = jnp.dot(weights, vals[...], preferred_element_type=F32)
        total = acc[:, HD:]
        o_ref[0, pl.ds(i * sub, sub), :] = (acc[:, :HD] / total).astype(BF)
        lse = high + jnp.log2(total)
        for k in range(sub // 128):
            lse_rows.append(jnp.transpose(lse[k * 128 : (k + 1) * 128])[:1])
        current = later
    store_lse(o_ref, jnp.concatenate(lse_rows, axis=0))


def attention(part, place, queries, own, other):
    half = own.shape[0]
    whole = pl.BlockSpec((half, 2 * HD), lambda i, place: (0, 0))
    rows = pl.BlockSpec((QROWS, HD), lambda i, place: (part, 0))
    return pl.pallas_call(
        functools.partial(attention_body, 256),
        grid_spec=pltpu.PrefetchScalarGridSpec(
            num_scalar_prefetch=1,
            grid=(4,),
            in_specs=[rows] * 4 + [whole, whole],
            out_specs=pl.BlockSpec(
                (1, QROWS + 16, HD), lambda i, place: (place[0] ^ i, 0, 0)
            ),
            scratch_shapes=[pltpu.VMEM((2 * half, 2 * HD), BF)] * 2
            + [pltpu.VMEM((QROWS, HD), BF)],
        ),
        out_shape=jax.ShapeDtypeStruct((4, QROWS + 16, HD), BF),
        compiler_params=pltpu.CompilerParams(vmem_limit_bytes=32 * MIB),
        cost_estimate=pl.CostEstimate(
            flops=4 * 4 * QROWS * 2 * half * 2 * HD,
            bytes_accessed=4 * MIB,
            transcendentals=4 * QROWS * 2 * half,
        ),
        name="attention",
    )(place, *queries, own, other)


def merge_two_body(a_ref, b_ref, o_ref):
    la, lb = load_lse(a_ref, 0), load_lse(b_ref, 0)
    high = jnp.maximum(la, lb)
    ea, eb = jnp.exp2(la - high), jnp.exp2(lb - high)
    total = ea + eb
    store_lse(o_ref, high + jnp.log2(total))
    ea, eb = ea / total, eb / total
    for k in range(4):
        span = pl.ds(k * 128, 128)
        mixed = column(ea[k : k + 1]) * a_ref[0, span, :].astype(F32)
        mixed = mixed + column(eb[k : k + 1]) * b_ref[0, span, :].astype(F32)
        o_ref[0, span, :] = mixed.astype(BF)


def merge_two(a, b):
    block = pl.BlockSpec((1,) + a.shape[1:], lambda i: (i, 0, 0))
    return pl.pallas_call(
        merge_two_body,
        grid=(a.shape[0],),
        in_specs=[block, block],
        out_specs=block,
        out_shape=jax.ShapeDtypeStruct(a.shape, BF),
        name="merge_two",
    )(a, b)


def merge_body(part_ref, o_ref):
    count = part_ref.shape[0]
    lses = [load_lse(part_ref, s) for s in range(count)]
    high = functools.reduce(jnp.maximum, lses)
    shares = [jnp.exp2(v - high) for v in lses]
    total = functools.reduce(jnp.add, shares)
    shares = [v / total for v in shares]
    for k in range(4):
        acc = jnp.zeros((128, HD), F32)
        for s in range(count):
            part = part_ref[s, pl.ds(k * 128, 128), :].astype(F32)
            acc = acc + column(shares[s][k : k + 1]) * part
        acc = acc.astype(BF)
        for n in range(4):
            o_ref[k * 4 + n] = acc[n // 2 * 64 : n // 2 * 64 + 64]


def merge(parts):
    return ones_call(merge_body, jax.ShapeDtypeStruct((N, 64, HD), BF), name="merge")(parts)


def bf16_terms(v):
    hi = v.astype(BF).astype(F32)
    mid = (v - hi).astype(BF).astype(F32)
    return [hi, mid, v - hi - mid]


def project_body(
    pos_ref, att_ref, wa_ref, wb_ref, scale_ref, shift_ref, fw_ref, fb_ref, *refs
):
    own_ref, send_ref, const_ref, rows, x, stats = refs
    step = pl.program_id(0)
    core, side = pos_ref[0], pos_ref[1]
    cols = wa_ref.shape[1]
    half = D // 2
    contract = (((1,), (1,)), ((), ()))

    @pl.when(step == 0)
    def _():
        for h in range(HEADS):
            rows[:, h * HD : (h + 1) * HD] = att_ref[h]
        moved = jnp.zeros((1, 128), F32)
        blank = jnp.zeros((64, half), BF)
        for s in range(2):
            span = pl.ds(s * half, half)
            terms = bf16_terms(1.0 + scale_ref[:, span]) + bf16_terms(shift_ref[:, span])
            lhs = jnp.concatenate(terms + [jnp.zeros((2, half), F32)], axis=0).astype(BF)
            rhs = jnp.concatenate([fw_ref[:, span], blank], axis=0)
            got = lax.dot_general(lhs, rhs, contract, preferred_element_type=F32)
            const_ref[s : s + 1, :] = got[0:1] + got[1:2] + got[2:3]
            moved = moved + got[3:4] + got[4:5] + got[5:6]
        const_ref[2:3, :] = moved + fb_ref[...]

    a = rows[...]
    x[core, step] = jnp.dot(a, wa_ref[...], preferred_element_type=F32)
    x[1 - core, step] = jnp.dot(a, wb_ref[...], preferred_element_type=F32)

    @pl.when(step == pl.num_programs(0) - 1)
    def _():
        parts = [x[s, i] for s in range(2) for i in range(x.shape[1])]
        mean = sum(jnp.sum(p, axis=1, keepdims=True) for p in parts) * (1.0 / half)
        parts = [p - mean for p in parts]
        square = sum(jnp.sum(p * p, axis=1, keepdims=True) for p in parts)
        acc = jnp.zeros(stats.shape, F32)
        blank = jnp.zeros((64, cols), BF)
        for n, p in enumerate(parts):
            span = pl.ds(pl.multiple_of(side * half, 128) + n * cols, cols)
            m = (p * (1.0 + scale_ref[:, span])).astype(BF)
            rhs = jnp.concatenate([fw_ref[:, span], blank], axis=0)
            acc = acc + lax.dot_general(m, rhs, contract, preferred_element_type=F32)
        lane = lax.broadcasted_iota(jnp.int32, stats.shape, 1)
        stats[...] = jnp.where(lane < 64, acc, jnp.where(lane < 96, mean, square))
        own_ref[...] = stats[pl.ds(pl.multiple_of(side * 32, 32), 32), :]
        send_ref[...] = stats[pl.ds(pl.multiple_of(32 - side * 32, 32), 32), :]


def project(pos, att, wa, wb, scale, shift, fw, fb):
    cols = 384
    steps = wa.shape[1] // cols
    block = pl.BlockSpec((HEADS * HD, cols), lambda i: (0, i))

    def whole(shape):
        return pl.BlockSpec(shape, lambda i: (0,) * len(shape))

    count = att.shape[1]
    outs = [(32, 128), (32, 128), (8, 128)]
    return pl.pallas_call(
        project_body,
        grid=(steps,),
        in_specs=[
            pl.BlockSpec(memory_space=pltpu.SMEM),
            whole(att.shape),
            block,
            block,
            whole(scale.shape),
            whole(shift.shape),
            whole(fw.shape),
            whole(fb.shape),
        ],
        out_specs=[whole(o) for o in outs],
        out_shape=[jax.ShapeDtypeStruct(o, F32) for o in outs],
        scratch_shapes=[
            pltpu.VMEM((count, HEADS * HD), BF),
            pltpu.VMEM((2, steps, count, cols), F32),
            pltpu.VMEM((count, 128), F32),
        ],
        compiler_params=pltpu.CompilerParams(vmem_limit_bytes=32 * MIB),
        name="project",
    )(pos, att, wa, wb, scale, shift, fw, fb)


def finish_body(pos_ref, own_ref, got_ref, const_ref, o_ref):
    side = pos_ref[1]
    own, got = own_ref[...], got_ref[...]
    m_own, m_got = own[:, 64:65], got[:, 64:65]
    apart = m_own - m_got
    square = own[:, 96:97] + got[:, 96:97] + apart * apart * (D / 4)
    rstd = lax.rsqrt(square * (1.0 / D) + NORM_EPS)
    first, second = const_ref[0:1, :], const_ref[1:2, :]
    u_own = jnp.where(side == 0, first, second)
    u_got = jnp.where(side == 0, second, first)
    total = own + got + (0.5 * apart) * (u_own - u_got)
    out = (total * rstd + const_ref[2:3, :]).astype(BF)[:, :64]

    src = lax.broadcasted_iota(jnp.int32, (64, 128), 0)
    dst = lax.broadcasted_iota(jnp.int32, (64, 128), 1)
    place = (src % 2) * 32 + (src // 2 % 2) * 16 + src // 4
    to = lax.broadcasted_iota(jnp.int32, (16, 32), 0)
    row = lax.broadcasted_iota(jnp.int32, (16, 32), 1)
    acc = jnp.zeros((16, 128), F32)
    for j in range(2):
        perm = jnp.where(dst == place + 64 * j, 1.0, 0.0).astype(BF)
        pick = jnp.where(row == (to % 8 * 2 + to // 8) * 2 + j, 1.0, 0.0).astype(BF)
        lanes = jnp.dot(out, perm, preferred_element_type=F32).astype(BF)
        acc = acc + jnp.dot(pick, lanes, preferred_element_type=F32)
    o_ref[...] = acc.astype(BF)


def finish(pos, own, got, const):
    vmem = pl.BlockSpec(memory_space=pltpu.VMEM)
    return pl.pallas_call(
        finish_body,
        in_specs=[pl.BlockSpec(memory_space=pltpu.SMEM), vmem, vmem, vmem],
        out_shape=jax.ShapeDtypeStruct((16, 128), BF),
        name="finish",
    )(pos, own, got, const)


def conv_body(blk_ref, r_ref, k1_ref, b1_ref, k2_ref, b2_ref, o_ref, win, feat, w1, w2):
    blank = jnp.zeros((16, CH), BF)
    for a in range(3):
        for wr in range(4):
            for wc in range(4):
                ry, p = divmod(wr, 2)
                row = ((a * 2 + ry) * 4 + wc) * 32 + p * 16
                for ey in range(2):
                    for ex in range(2):
                        b, g = wr - ey, wc - ex
                        hit = 0 <= b < 3 and 0 <= g < 3
                        tile = k1_ref[(a * 3 + b) * 3 + g] if hit else blank
                        w1[pl.ds(row, 16), pl.ds((ey * 2 + ex) * CH, CH)] = tile
    taps = ((1, 0, None, 2), (2, 1, 0, None))
    blank = jnp.zeros((32, CH), BF)
    for a in range(3):
        for u, pair in enumerate(((2, None), (1, 2), (0, 1), (None, 0))):
            for ey, b in enumerate(pair):
                for qi in range(2):
                    for n, g in enumerate(taps[qi]):
                        hit = b is not None and g is not None
                        tile = k2_ref[(a * 3 + b) * 3 + g] if hit else blank
                        span = pl.ds((ey * 2 + qi) * CH, CH)
                        w2[a, pl.ds(u * 128 + n * 32, 32), span] = tile

    rows = r_ref[...].astype(F32).reshape(512, 128)
    lane = lax.broadcasted_iota(jnp.int32, (512, 128), 1)
    col = lax.broadcasted_iota(jnp.int32, (512, 128), 0) % 16
    before = jnp.where(col == 0, 0.0, pltpu.roll(rows, 1, 0))
    after = jnp.where(col == 15, 0.0, pltpu.roll(rows, 511, 0))
    views = (
        pltpu.roll(jnp.where(lane < 96, rows, before), 32, 1),
        pltpu.roll(jnp.where(lane < 32, after, rows), 96, 1),
    )
    for j, view in enumerate(views):
        view = view.astype(BF).reshape(4, 8, 16, 128)
        for r in range(3):
            for ry in range(2):
                span = pl.ds(ry * 128, 128)
                win[j, 2:, r, :, span] = view[r + ry]
                for early in range(2):
                    win[j, early, r, :, span] = view[r + ry, 0]

    top = jnp.where(blk_ref[0] == 0, 0.0, 1.0)
    bottom = jnp.where(blk_ref[0] == N - 1, 0.0, 1.0)
    for j in range(2):
        lhs = jnp.concatenate([win[j, a : a + 8] for a in range(3)], axis=-1)
        lhs = lhs.reshape(8 * 3 * 16, lhs.shape[-1])
        for n in range(4):
            span = pl.ds(n * CH, CH)
            v = jnp.dot(lhs, w1[:, span], preferred_element_type=F32) + b1_ref[...]
            v = (v / (1.0 + jnp.exp(-v))).reshape(8, 3, 16, CH)
            for r in range(3):
                f = v[:, r]
                if (r, n // 2) == (0, 0):
                    f = f * top
                if (r, n // 2) == (2, 1):
                    f = f * bottom
                f = f.astype(BF)
                feat[j, 2:, r, :, span] = f
                feat[j, 0, r, :, span] = f[0]
                feat[j, 1, r, :, span] = f[0]

    def product(a, r, first):
        lhs = feat[:, a : a + 8, r].reshape(256, 4 * CH)
        rhs = w2[a, pl.ds(first, 256), :]
        return lax.dot_general(lhs, rhs, (((1,), (1,)), ((), ())), preferred_element_type=F32)

    lane = lax.broadcasted_iota(jnp.int32, (128, 128), 1)
    col = lax.broadcasted_iota(jnp.int32, (128, 128), 0) % 16
    for pair in range(2):
        acc = jnp.zeros((256, 256), F32)
        for a in range(3):
            acc = acc + product(a, pair, 256) + product(a, pair + 1, 0)
        for y in range(2):
            z = acc[:, y * 128 : (y + 1) * 128]
            z0, z1 = z[:128], z[128:]
            right = jnp.where(col == 0, 0.0, pltpu.roll(z1, 1, 0))
            left = jnp.where(col == 15, 0.0, pltpu.roll(z0, 127, 0))
            s0 = z0 + pltpu.roll(jnp.where(lane < 96, right, z1), 64, 1)
            s1 = z1 + pltpu.roll(jnp.where(lane < 96, z0, left), 64, 1)
            out = jnp.where(lane < 64, s0, pltpu.roll(s1, 64, 1)) + b2_ref[...]
            o_ref[pair * 2 + y] = out.astype(BF).reshape(8, 16, 128)


def conv_stage(blk, rows, k1, b1, k2, b2):
    vmem = pl.BlockSpec(memory_space=pltpu.VMEM)
    return pl.pallas_call(
        conv_body,
        in_specs=[pl.BlockSpec(memory_space=pltpu.SMEM)] + [vmem] * 5,
        out_shape=jax.ShapeDtypeStruct((4, 8, 16, 128), BF),
        scratch_shapes=[
            pltpu.VMEM((2, 10, 3, 16, 256), BF),
            pltpu.VMEM((2, 10, 3, 16, 4 * CH), BF),
            pltpu.VMEM((768, 4 * CH), BF),
            pltpu.VMEM((3, 512, 4 * CH), BF),
        ],
        compiler_params=pltpu.CompilerParams(vmem_limit_bytes=32 * MIB),
        name="convs",
    )(blk, rows, k1, b1, k2, b2)


def after(value, *others):
    return lax.optimization_barrier((value,) + others)[0]


def shards(
    qkv,
    query_blocks,
    out_weight,
    mod_shift,
    mod_scale,
    final_weight,
    final_bias,
    conv_in_weight,
    conv_in_bias,
    conv_weight,
    conv_bias,
):
    head = lax.axis_index("head")
    blk = lax.axis_index("blk")
    core = blk % 2
    side = head % 2
    pos = jnp.stack([core, side])

    q_send, kv_send = split_heads(qkv)
    q_all = lax.all_to_all(q_send, "head", 0, 0, tiled=True)
    kv_own = lax.all_to_all(after(kv_send, q_all), "head", 0, 0, tiled=True)
    kv_own = kv_own.reshape(-1, 2 * HD)

    near = select_queries(query_blocks, q_all)
    both = jnp.concatenate([near, lax.ppermute(near, "blk", FAR_SWAP)], axis=0)
    queries = [both]
    for m in range(1, 4):
        swap = [(i, i ^ (2 * m)) for i in range(N)]
        queries.append(lax.ppermute(both, "blk", swap))
    kv_own = after(kv_own, *queries)
    kv_other = lax.ppermute(kv_own, "blk", NEXT_SWAP)

    quarter = D // 4
    mine, theirs = (side * 2 + core) * quarter, ((1 - side) * 2 + core) * quarter
    source = after(out_weight, q_send)
    part = lax.dynamic_slice_in_dim(source, mine, quarter, axis=1)
    given = lax.dynamic_slice_in_dim(source, theirs, quarter, axis=1)
    given = after(lax.ppermute(given, "head", NEXT_SWAP), q_all)
    pair = jnp.stack([jnp.where(side == 0, part, given), jnp.where(side == 0, given, part)])
    weight_a = lax.all_gather(pair, "head", axis=0, tiled=True, axis_index_groups=GROUPS_Z)

    place = (blk // 2 % 4).reshape(1)
    far_part = attention(1, place, queries, kv_own, kv_other)
    got_part = lax.ppermute(far_part, "blk", FAR_SWAP)
    near_part = attention(0, after(place, far_part), queries, kv_own, kv_other)
    partial = merge_two(near_part, got_part)

    weight_a = after(weight_a, far_part).reshape(HEADS * HD, quarter)
    weight_b = lax.ppermute(weight_a, "blk", NEXT_SWAP)

    partial = lax.all_to_all(partial, "blk", 0, 0, tiled=True, axis_index_groups=GROUPS_Y)
    attended = lax.all_to_all(merge(partial), "head", 0, 0, tiled=True)
    own, send, const = project(
        pos,
        attended,
        weight_a,
        weight_b,
        mod_scale.reshape(1, D),
        mod_shift.reshape(1, D),
        jnp.transpose(final_weight),
        jnp.pad(final_bias, (0, 64)).reshape(1, 128),
    )
    tile = finish(pos, own, lax.ppermute(send, "head", NEXT_SWAP), const)

    ends = N - 1
    above = lax.ppermute(tile[8:], "blk", [(i, i + 1) for i in range(ends)])
    below = lax.ppermute(tile[:8], "blk", [(i + 1, i) for i in range(ends)])
    rows = jnp.concatenate([above, tile, below], axis=0)
    rows = lax.all_to_all(
        jnp.broadcast_to(rows[None], (N,) + rows.shape), "head", 0, 0, tiled=True
    )
    bias_out = lax.dynamic_slice_in_dim(conv_bias, head * 32, 32)
    out = conv_stage(
        blk.reshape(1),
        jnp.transpose(rows, (1, 0, 2)),
        conv_in_weight.reshape(27, 16, CH),
        conv_in_bias.reshape(1, CH),
        jnp.transpose(conv_weight, (0, 1, 2, 4, 3)).reshape(27, 32, CH),
        jnp.tile(bias_out, 4).reshape(1, -1),
    )
    out = lax.all_to_all(jnp.transpose(out, (2, 0, 1, 3)), "head", 0, 0, tiled=True)
    out = jnp.transpose(out.reshape(N, 4, 8, 4, 32), (2, 1, 3, 0, 4))
    return out.reshape(8, 4, 4, CH)


def solution(mesh):
    in_specs = (
        P("blk", "head", None),
        P("blk"),
        P("head", None),
        P(),
        P(),
        P(),
        P(),
        P(),
        P(),
        P(None, None, None, None, "head"),
        P(),
    )
    out_specs = P(None, "blk", "head", None)
    return jax.shard_map(shards, mesh=mesh, in_specs=in_specs, out_specs=out_specs, check_vma=False)
```

time: 325 us -> 217 us (0.67)
  waiting for transfers between devices: 142 us -> 82.7 us
  local copies, waits for them, and re-layouts: 51.4 us -> 13 us
  blocking collectives: 14.1 us -> 26.3 us
  other arithmetic: 15.4 us -> 3.67 us
  Pallas kernels: 47.9 us -> 41.8 us
  starting transfers between devices: 39.4 us -> 35 us
    all_gather x1, waiting for transfers between devices: 77.6 us -> 4.69 us  [shards(): lax.all_gather(pair, 'head', axis=0, tiled=True, axis_index_groups=GROUPS_Z)]
    reshape x10 -> x1, local copies, waits for them, and re-layouts: 26.4 us -> 0.01 us  [shards(): jnp.pad(final_bias, (0, 64)).reshape(1, 128)]
    ppermute x5 -> x11, waiting for transfers between devices: 14.4 us -> 39.9 us  [the longest x3 12.2 us: shards(): queries.append(lax.ppermute(both, 'blk', swap))]
    all_to_all x4 -> x2, starting transfers between devices: 25.3 us -> 9.19 us  [the longest x1 5.52 us: shards(): attended = lax.all_to_all(merge(partial), 'head', 0, 0, tiled=True)]
    all_to_all x0 -> x1, blocking collectives: none -> 14 us  [shards(): lax.all_to_all(partial, 'blk', 0, 0, tiled=True, axis_index_groups=GROUPS_Y)]
    all_to_all x1, waiting for transfers between devices: 17.5 us -> 8.58 us  [shards(): q_all = lax.all_to_all(q_send, 'head', 0, 0, tiled=True)]
    all_to_all x4 -> x2, waiting for transfers between devices: 29 us -> 20.7 us  [the longest x1 10.9 us: shards(): attended = lax.all_to_all(merge(partial), 'head', 0, 0, tiled=True)]
    ppermute x5 -> x11, starting transfers between devices: 5.62 us -> 13 us  [the longest x3 4.79 us: shards(): queries.append(lax.ppermute(both, 'blk', swap))]
  transfers between devices with their start and end apart: 12 -> 16, of which waited for: 8 -> 14; matrix products, arithmetic and copies ran while one was open for 18% -> 1% of each run, Pallas kernels for 8% -> 13%
where the time goes in v2:
time: 217 us; the launch traced here: 216 us
  waiting for transfers between devices  82.7 us (38%)
  Pallas kernels  41.8 us (19%)
  starting transfers between devices  35 us (16%)
  blocking collectives  26.3 us (12%)
  between operations  13.7 us (6%)
  local copies, waits for them, and re-layouts  13 us (6%)
  other arithmetic  3.67 us (2%)
    pallas_call x2, Pallas kernels, attention(): pl.pallas_call(functools.partial(attention_body, 256), grid_spec=pltpu.Pr...  22.9 us
    all_to_all x1, blocking collectives, shards(): lax.all_to_all(partial, 'blk', 0, 0, tiled=True, axis_index_groups=GROUPS_Y)  14 us
    all_to_all x1, blocking collectives, shards(): lax.all_to_all(jnp.transpose(out, (2, 0, 1, 3)), 'head', 0, 0, tiled=True)  12.3 us
    ppermute x3, waiting for transfers between devices, shards(): queries.append(lax.ppermute(both, 'blk', swap))  12.2 us
    all_to_all x1, waiting for transfers between devices, shards(): attended = lax.all_to_all(merge(partial), 'head', 0, 0, tiled=True)  10.9 us
    all_to_all x1, waiting for transfers between devices, shards(): kv_own = lax.all_to_all(after(kv_send, q_all), 'head', 0, 0, tiled=True)  9.84 us
    all_to_all x1, starting transfers between devices, shards(): q_all = lax.all_to_all(q_send, 'head', 0, 0, tiled=True)  9.2 us
    all_to_all x1, waiting for transfers between devices, shards(): lax.all_to_all(jnp.broadcast_to(rows[None], (N,) + rows.shape), 'head', 0...  8.8 us
  transfers between devices with their start and end apart: 16, of which 14 were waited for; matrix products, arithmetic and copies ran while one was open for 1% of the time, Pallas kernels for 13%

profile of v2, /device:TPU:4, one launch (start us, length us, event | category | flops | bytes accessed | tf_op | source)
XLA Modules:
  0.0 216.2 jit_solution(10955808860571247374)
XLA Ops:
  9.4 9.2 %all-to-all-start = ((bf16[16,128,128]{2,1,0:T(8,128)(2,1)}), bf16[16,128,128]{2,1,0:T(8,128)(2,1)S(1)}, u32[]{:S(2)}, u32[]{:S(2)}) async-start(bf16[16,128,128]{2,1,0:T(8,128)(2,1)} %get-tuple-element.16), calls=%async_computation | async-start | bytes 1048576 | tf_op jit(solution)/shard_map/all_to_all | solution.py:460
  19.6 2.0 collective-permute-start.6
  21.6 5.5 %collective-permute-done.6 = bf16[128,768]{1,0:T(8,128)(2,1)S(1)} collective-permute-done((bf16[128,768]{1,0:T(8,128)(2,1)S(1)}, bf16[128,768]{1,0:T(8,128)(2,1)S(1)}, u32[]{:S(2)}, u32[]{:S(2)}) %collective-permute-start.6) | collective-permute-done | bytes 196640 | tf_op jit(solution)/shard_map/ppermute | solution.py:478
  27.2 8.6 %all-to-all-done.q_ref = bf16[16,128,128]{2,1,0:T(8,128)(2,1)S(1)} async-done(((bf16[16,128,128]{2,1,0:T(8,128)(2,1)}), bf16[16,128,128]{2,1,0:T(8,128)(2,1)S(1)}, u32[]{:S(2)}, u32[]{:S(2)}) %all-to-all-start) | async-done | bytes 524320 | tf_op jit(solution)/shard_map/all_to_all | solution.py:460
  37.8 3.7 %all-to-all-start.1 = ((bf16[16,128,256]{2,1,0:T(8,128)(2,1)}), bf16[16,128,256]{2,1,0:T(8,128)(2,1)S(1)}, u32[]{:S(2)}, u32[]{:S(2)}) async-start(bf16[16,128,256]{2,1,0:T(8,128)(2,1)} %get-tuple-element.18), calls=%async_computation.1 | async-start | bytes 2097152 | tf_op jit(solution)/shard_map/all_to_all | solution.py:461
  41.5 1.7 select.12
  44.0 6.2 %collective-permute-done = bf16[512,128]{1,0:T(8,128)(2,1)S(1)} collective-permute-done((bf16[512,128]{1,0:T(8,128)(2,1)}, bf16[512,128]{1,0:T(8,128)(2,1)S(1)}, u32[]{:S(2)}, u32[]{:S(2)}) %collective-permute-start) | collective-permute-done | bytes 131104 | tf_op jit(solution)/shard_map/ppermute | solution.py:465
  51.1 1.7 collective-permute-start.1
  52.8 2.9 %collective-permute-start.2 = (bf16[1024,128]{1,0:T(8,128)(2,1)S(1)}, bf16[1024,128]{1,0:T(8,128)(2,1)S(1)}, u32[]{:S(2)}, u32[]{:S(2)}) collective-permute-start(bf16[1024,128]{1,0:T(8,128)(2,1)S(1)} %pad_maximum_fusion.1.refs_0_), channel_id=1, source_target_pairs={{0,4},{1,5},{2,6},{3,7},{4,0},{5,1},{6,2},{7,3},{8,12},{9,13},{10,... | collective-permute-start | bytes 786440 | tf_op jit(solution)/shard_map/ppermute | solution.py:469
  55.9 4.3 %collective-permute-done.1.refs_1_ = bf16[1024,128]{1,0:T(8,128)(2,1)S(1)} collective-permute-done((bf16[1024,128]{1,0:T(8,128)(2,1)S(1)}, bf16[1024,128]{1,0:T(8,128)(2,1)S(1)}, u32[]{:S(2)}, u32[]{:S(2)}) %collective-permute-start.1) | collective-permute-done | bytes 262176 | tf_op jit(solution)/shard_map/ppermute | solution.py:469
  60.2 5.3 %collective-permute-done.2.refs_2_ = bf16[1024,128]{1,0:T(8,128)(2,1)S(1)} collective-permute-done((bf16[1024,128]{1,0:T(8,128)(2,1)S(1)}, bf16[1024,128]{1,0:T(8,128)(2,1)S(1)}, u32[]{:S(2)}, u32[]{:S(2)}) %collective-permute-start.2) | collective-permute-done | bytes 262176 | tf_op jit(solution)/shard_map/ppermute | solution.py:469
  65.5 2.6 %collective-permute-done.3.refs_3_ = bf16[1024,128]{1,0:T(8,128)(2,1)S(1)} collective-permute-done((bf16[1024,128]{1,0:T(8,128)(2,1)S(1)}, bf16[1024,128]{1,0:T(8,128)(2,1)S(1)}, u32[]{:S(2)}, u32[]{:S(2)}) %collective-permute-start.3) | collective-permute-done | bytes 262176 | tf_op jit(solution)/shard_map/ppermute | solution.py:469
  68.2 9.8 %all-to-all-done.1 = bf16[16,128,256]{2,1,0:T(8,128)(2,1)S(1)} async-done(((bf16[16,128,256]{2,1,0:T(8,128)(2,1)}), bf16[16,128,256]{2,1,0:T(8,128)(2,1)S(1)}, u32[]{:S(2)}, u32[]{:S(2)}) %all-to-all-start.1) | async-done | bytes 1048608 | tf_op jit(solution)/shard_map/all_to_all | solution.py:461
  78.0 2.7 %collective-permute-done.4.refs_5_ = bf16[2048,256]{1,0:T(8,128)(2,1)S(1)} collective-permute-done((bf16[2048,256]{1,0:T(8,128)(2,1)S(1)}, bf16[2048,256]{1,0:T(8,128)(2,1)S(1)}, u32[]{:S(2)}, u32[]{:S(2)}) %collective-permute-start.4) | collective-permute-done | bytes 1048608 | tf_op jit(solution)/shard_map/ppermute | solution.py:471
  80.7 11.8 %attention.2 = bf16[4,528,128]{2,1,0:T(8,128)(2,1)} custom-call(s32[1]{0:T(128)} %bitcast.3.place_ref, bf16[1024,128]{1,0:T(8,128)(2,1)S(1)} %pad_maximum_fusion.1.refs_0_, bf16[1024,128]{1,0:T(8,128)(2,1)S(1)} %collective-permute-done.1.refs_1_, bf16[1024,128]{1,0:T(8,128)(2,1)S(1)} %collective-permute-done.2.refs_2_, ...), custom_call_target="tpu_custom_call" | custom-call | flops 8589934592 | bytes 4194304 | tf_op jit(solution)/shard_map/attention/pallas_call | solution.py:137
  92.5 4.7 %all-gather.2.cloned.1.call-done = bf16[16,128,768]{2,1,0:T(8,128)(2,1)} async-done(((bf16[2,128,768]{2,1,0:T(8,128)(2,1)}), bf16[16,128,768]{2,1,0:T(8,128)(2,1)}) %all-gather.2.cloned.1.call-update) | async-done | bytes 3145744 | tf_op jit(solution)/shard_map/all_gather | solution.py:480
  97.9 11.1 %attention.3.a_ref = bf16[4,528,128]{2,1,0:T(8,128)(2,1)S(1)} custom-call(s32[1]{0:T(128)} %bitcast.3.place_ref, bf16[1024,128]{1,0:T(8,128)(2,1)S(1)} %pad_maximum_fusion.1.refs_0_, bf16[1024,128]{1,0:T(8,128)(2,1)S(1)} %collective-permute-done.1.refs_1_, bf16[1024,128]{1,0:T(8,128)(2,1)S(1)} %collective-permute-done.2.refs_2_, ...), custom_call_target="tpu_custom_call" | custom-call | flops 8589934592 | bytes 4194304 | tf_op jit(solution)/shard_map/attention/pallas_call | solution.py:137
  109.9 3.8 %collective-permute-done.5.b_ref = bf16[4,528,128]{2,1,0:T(8,128)(2,1)} collective-permute-done((bf16[4,528,128]{2,1,0:T(8,128)(2,1)}, bf16[4,528,128]{2,1,0:T(8,128)(2,1)}, u32[]{:S(2)}, u32[]{:S(2)}) %collective-permute-start.5) | collective-permute-done | bytes 540704 | tf_op jit(solution)/shard_map/ppermute | solution.py:484
  113.7 3.7 %merge_two.1 = bf16[4,528,128]{2,1,0:T(8,128)(2,1)} custom-call(bf16[4,528,128]{2,1,0:T(8,128)(2,1)} %copy-done.4, bf16[4,528,128]{2,1,0:T(8,128)(2,1)} %collective-permute-done.5.b_ref), custom_call_target="tpu_custom_call" | custom-call | tf_op jit(solution)/shard_map/merge_two/pallas_call | solution.py:176
  117.4 14.0 %all_to_all.30.part_ref = bf16[4,528,128]{2,1,0:T(8,128)(2,1)S(1)} all-to-all(bf16[4,528,128]{2,1,0:T(8,128)(2,1)} %merge_two.1), channel_id=1, replica_groups={{0,2,4,6},{1,3,5,7},{8,10,12,14},{9,11,13,15},{16,18,20,22},{17,19,21,2..., dimensions={0} | all-to-all | bytes 1081344 | tf_op jit(solution)/shard_map/all_to_all | solution.py:491
  132.5 5.5 %all-to-all-start.3 = ((bf16[16,64,128]{2,1,0:T(8,128)(2,1)}), bf16[16,64,128]{2,1,0:T(8,128)(2,1)S(1)}, u32[]{:S(2)}, u32[]{:S(2)}) async-start(bf16[16,64,128]{2,1,0:T(8,128)(2,1)} %copy-done.2), calls=%async_computation.3 | async-start | bytes 524288 | tf_op jit(solution)/shard_map/all_to_all | solution.py:492
  138.1 10.9 %all-to-all-done.3.att_ref = bf16[16,64,128]{2,1,0:T(8,128)(2,1)S(1)} async-done(((bf16[16,64,128]{2,1,0:T(8,128)(2,1)}), bf16[16,64,128]{2,1,0:T(8,128)(2,1)S(1)}, u32[]{:S(2)}, u32[]{:S(2)}) %all-to-all-start.3) | async-done | bytes 262176 | tf_op jit(solution)/shard_map/all_to_all | solution.py:492
  150.0 3.5 %project.1 = (f32[32,128]{1,0:T(8,128)S(1)}, f32[32,128]{1,0:T(8,128)S(1)}, f32[8,128]{1,0:T(8,128)S(1)}) custom-call(s32[2]{0:T(128)S(1)} %pad_add_fusion.pos_ref, bf16[16,64,128]{2,1,0:T(8,128)(2,1)S(1)} %all-to-all-done.3.att_ref, bf16[2048,768]{1,0:T(8,128)(2,1)S(1)} %bitcast.30, bf16[2048,768]{1,0:T(8,128)(2,1)} %collective-permute-done.7.wb_ref, ...), custom_call_target="tpu_custom_call" | custom-call | tf_op jit(solution)/shard_map/project/pallas_call | solution.py:272
  155.0 3.4 %collective-permute-done.8.got_ref = f32[32,128]{1,0:T(8,128)S(1)} collective-permute-done((f32[32,128]{1,0:T(8,128)S(1)}, f32[32,128]{1,0:T(8,128)S(1)}, u32[]{:S(2)}, u32[]{:S(2)}) %collective-permute-start.8) | collective-permute-done | bytes 16416 | tf_op jit(solution)/shard_map/ppermute | solution.py:503
  159.0 1.8 finish.1
  161.5 1.9 collective-permute-start.10
  163.4 2.4 %collective-permute-start.9 = (bf16[8,128]{1,0:T(8,128)(2,1)S(1)}, bf16[8,128]{1,0:T(8,128)(2,1)S(1)}, u32[]{:S(2)}, u32[]{:S(2)}) collective-permute-start(bf16[8,128]{1,0:T(8,128)(2,1)S(1)} %get-tuple-element.29), channel_id=1, source_target_pairs={{0,1},{1,2},{2,3},{3,4},{4,5},{5,6},{6,7},{7,8},{8,9},{9,10},{10,1... | collective-permute-start | bytes 6152 | tf_op jit(solution)/shard_map/ppermute | solution.py:506
  165.8 6.1 %collective-permute-done.9 = bf16[8,128]{1,0:T(8,128)(2,1)S(1)} collective-permute-done((bf16[8,128]{1,0:T(8,128)(2,1)S(1)}, bf16[8,128]{1,0:T(8,128)(2,1)S(1)}, u32[]{:S(2)}, u32[]{:S(2)}) %collective-permute-start.9) | collective-permute-done | bytes 2080 | tf_op jit(solution)/shard_map/ppermute | solution.py:506
  173.3 3.5 %all-to-all-start.4 = ((bf16[16,32,128]{2,1,0:T(8,128)(2,1)}), bf16[16,32,128]{2,1,0:T(8,128)(2,1)S(1)}, u32[]{:S(2)}, u32[]{:S(2)}) async-start(bf16[16,32,128]{2,1,0:T(8,128)(2,1)} %broadcast_in_dim.2), calls=%async_computation.4 | async-start | bytes 262144 | tf_op jit(solution)/shard_map/all_to_all | solution.py:509
  177.7 8.8 %all-to-all-done.4 = bf16[16,32,128]{2,1,0:T(8,128)(2,1)S(1)} async-done(((bf16[16,32,128]{2,1,0:T(8,128)(2,1)}), bf16[16,32,128]{2,1,0:T(8,128)(2,1)S(1)}, u32[]{:S(2)}, u32[]{:S(2)}) %all-to-all-start.4) | async-done | bytes 131104 | tf_op jit(solution)/shard_map/all_to_all | solution.py:509
  188.7 6.3 %convs.1 = bf16[4,8,16,128]{3,2,1,0:T(8,128)(2,1)S(1)} custom-call(s32[1]{0:T(128)} %bitcast.blk_ref, bf16[32,16,128]{2,1,0:T(8,128)(2,1)S(1)} %bitcast.35, bf16[27,16,512]{2,1,0:T(8,128)(2,1)S(1)} %bitcast.37, f32[1,512]{1,0:T(1,128)S(1)} %bitcast.41, bf16[27,32,512]{2,1,0:T(8,128)(2,1)S(1)} %bitcast.34, f32[1,128]{1,0:T(1,128)S(1)} %reshape_tile.3.b2_ref), custom_call_target="tpu_custom_call" | custom-call | tf_op jit(solution)/shard_map/convs/pallas_call | solution.py:421
  195.1 12.3 %all_to_all.31 = bf16[16,4,8,128]{3,2,1,0:T(8,128)(2,1)S(1)} all-to-all(bf16[16,4,8,128]{3,2,1,0:T(8,128)(2,1)S(1)} %copy.14), channel_id=1, replica_groups=mesh['head'=16,'blk'=16] {'head'}, dimensions={0} | all-to-all | bytes 262144 | tf_op jit(solution)/shard_map/all_to_all | solution.py:521
  (61 shorter events, 20.7 us)
Async XLA Ops:
  6.5 1.4 copy-start.1
  9.4 26.4 %all-to-all-start = ((bf16[16,128,128]{2,1,0:T(8,128)(2,1)}), bf16[16,128,128]{2,1,0:T(8,128)(2,1)S(1)}, u32[]{:S(2)}, u32[]{:S(2)}) async-start(bf16[16,128,128]{2,1,0:T(8,128)(2,1)} %get-tuple-element.16), calls=%async_computation | async-start | bytes 1048576 | tf_op jit(solution)/shard_map/all_to_all | solution.py:460
  18.6 78.5 %all-gather.2.cloned.1.call-start = ((), (), s32[]{:S(2)}) async-start(), calls=%async_computation.6 | async-start | bytes 3538944 | tf_op jit(solution)/shard_map/all_gather | solution.py:480
  19.6 7.6 %collective-permute-start.6 = (bf16[128,768]{1,0:T(8,128)(2,1)S(1)}, bf16[128,768]{1,0:T(8,128)(2,1)S(1)}, u32[]{:S(2)}, u32[]{:S(2)}) collective-permute-start(bf16[128,768]{1,0:T(8,128)(2,1)S(1)} %constant_dynamic-slice_fusion), channel_id=1, source_target_pairs={{0,16},{16,0},{32,48},{48,32},{64,80},{80,64},{96,112},{112,96},{1... | collective-permute-start | bytes 589832 | tf_op jit(solution)/shard_map/ppermute | solution.py:478
  35.8 5.7 %copy-start.13 = (bf16[16,128,128]{2,1,0:T(8,128)(2,1)}, bf16[16,128,128]{2,1,0:T(8,128)(2,1)S(1)}, u32[]{:S(2)}) copy-start(bf16[16,128,128]{2,1,0:T(8,128)(2,1)S(1)} %all-to-all-done.q_ref) | copy-start | bytes 1572868
  37.8 40.2 %all-to-all-start.1 = ((bf16[16,128,256]{2,1,0:T(8,128)(2,1)}), bf16[16,128,256]{2,1,0:T(8,128)(2,1)S(1)}, u32[]{:S(2)}, u32[]{:S(2)}) async-start(bf16[16,128,256]{2,1,0:T(8,128)(2,1)} %get-tuple-element.18), calls=%async_computation.1 | async-start | bytes 2097152 | tf_op jit(solution)/shard_map/all_to_all | solution.py:461
  43.2 7.0 %collective-permute-start = (bf16[512,128]{1,0:T(8,128)(2,1)}, bf16[512,128]{1,0:T(8,128)(2,1)S(1)}, u32[]{:S(2)}, u32[]{:S(2)}) collective-permute-start(bf16[512,128]{1,0:T(8,128)(2,1)} %select.12), channel_id=1, source_target_pairs={{0,8},{1,9},{2,10},{3,11},{4,12},{5,13},{6,14},{7,15},{8,0},{9,1},... | collective-permute-start | bytes 393224 | tf_op jit(solution)/shard_map/ppermute | solution.py:465
  51.1 9.1 %collective-permute-start.1 = (bf16[1024,128]{1,0:T(8,128)(2,1)S(1)}, bf16[1024,128]{1,0:T(8,128)(2,1)S(1)}, u32[]{:S(2)}, u32[]{:S(2)}) collective-permute-start(bf16[1024,128]{1,0:T(8,128)(2,1)S(1)} %pad_maximum_fusion.1.refs_0_), channel_id=1, source_target_pairs={{0,2},{1,3},{2,0},{3,1},{4,6},{5,7},{6,4},{7,5},{8,10},{9,11},{10,... | collective-permute-start | bytes 786440 | tf_op jit(solution)/shard_map/ppermute | solution.py:469
  52.8 12.7 %collective-permute-start.2 = (bf16[1024,128]{1,0:T(8,128)(2,1)S(1)}, bf16[1024,128]{1,0:T(8,128)(2,1)S(1)}, u32[]{:S(2)}, u32[]{:S(2)}) collective-permute-start(bf16[1024,128]{1,0:T(8,128)(2,1)S(1)} %pad_maximum_fusion.1.refs_0_), channel_id=1, source_target_pairs={{0,4},{1,5},{2,6},{3,7},{4,0},{5,1},{6,2},{7,3},{8,12},{9,13},{10,... | collective-permute-start | bytes 786440 | tf_op jit(solution)/shard_map/ppermute | solution.py:469
  55.7 12.5 %collective-permute-start.3 = (bf16[1024,128]{1,0:T(8,128)(2,1)S(1)}, bf16[1024,128]{1,0:T(8,128)(2,1)S(1)}, u32[]{:S(2)}, u32[]{:S(2)}) collective-permute-start(bf16[1024,128]{1,0:T(8,128)(2,1)S(1)} %pad_maximum_fusion.1.refs_0_), channel_id=1, source_target_pairs={{0,6},{1,7},{2,4},{3,5},{4,2},{5,3},{6,0},{7,1},{8,14},{9,15},{10,... | collective-permute-start | bytes 786440 | tf_op jit(solution)/shard_map/ppermute | solution.py:469
  78.0 2.7 %collective-permute-start.4 = (bf16[2048,256]{1,0:T(8,128)(2,1)S(1)}, bf16[2048,256]{1,0:T(8,128)(2,1)S(1)}, u32[]{:S(2)}, u32[]{:S(2)}) collective-permute-start(bf16[2048,256]{1,0:T(8,128)(2,1)S(1)} %bitcast.31), channel_id=1, source_target_pairs={{0,1},{1,0},{2,3},{3,2},{4,5},{5,4},{6,7},{7,6},{8,9},{9,8},{10,11... | collective-permute-start | bytes 3145736 | tf_op jit(solution)/shard_map/ppermute | solution.py:471
  97.1 51.8 %collective-permute-start.7 = (bf16[2048,768]{1,0:T(8,128)(2,1)}, bf16[2048,768]{1,0:T(8,128)(2,1)}, u32[]{:S(2)}, u32[]{:S(2)}) collective-permute-start(bf16[2048,768]{1,0:T(8,128)(2,1)} %bitcast.29), channel_id=1, source_target_pairs={{0,1},{1,0},{2,3},{3,2},{4,5},{5,4},{6,7},{7,6},{8,9},{9,8},{10,11... | collective-permute-start | bytes 9437192 | tf_op jit(solution)/shard_map/ppermute | solution.py:489
  97.1 16.5 %collective-permute-start.5 = (bf16[4,528,128]{2,1,0:T(8,128)(2,1)}, bf16[4,528,128]{2,1,0:T(8,128)(2,1)}, u32[]{:S(2)}, u32[]{:S(2)}) collective-permute-start(bf16[4,528,128]{2,1,0:T(8,128)(2,1)} %attention.2), channel_id=1, source_target_pairs={{0,8},{1,9},{2,10},{3,11},{4,12},{5,13},{6,14},{7,15},{8,0},{9,1},... | collective-permute-start | bytes 1622024 | tf_op jit(solution)/shard_map/ppermute | solution.py:484
  109.1 0.8 copy-start.4
  109.9 28.1 %copy-start.15 = (f32[64]{0:T(128)S(1)}, f32[64]{0:T(128)}, u32[]{:S(2)}) copy-start(f32[64]{0:T(128)} %param.17) | copy-start | bytes 772
  109.9 39.1 %copy-start = (bf16[16,128,768]{2,1,0:T(8,128)(2,1)S(1)}, bf16[16,128,768]{2,1,0:T(8,128)(2,1)}, u32[]{:S(2)}) copy-start(bf16[16,128,768]{2,1,0:T(8,128)(2,1)} %all-gather.2.cloned.1.call-done) | copy-start | bytes 9437188
  109.9 39.1 %copy-start.8 = (f32[3072]{0:T(1024)S(1)}, f32[3072]{0:T(1024)}, u32[]{:S(2)}) copy-start(f32[3072]{0:T(1024)} %param.15) | copy-start | bytes 36868
  109.9 39.1 %copy-start.9 = (f32[3072]{0:T(1024)S(1)}, f32[3072]{0:T(1024)}, u32[]{:S(2)}) copy-start(f32[3072]{0:T(1024)} %param.14) | copy-start | bytes 36868
  131.8 0.7 copy-start.2
  132.5 16.5 %all-to-all-start.3 = ((bf16[16,64,128]{2,1,0:T(8,128)(2,1)}), bf16[16,64,128]{2,1,0:T(8,128)(2,1)S(1)}, u32[]{:S(2)}, u32[]{:S(2)}) async-start(bf16[16,64,128]{2,1,0:T(8,128)(2,1)} %copy-done.2), calls=%async_computation.3 | async-start | bytes 524288 | tf_op jit(solution)/shard_map/all_to_all | solution.py:492
  138.1 15.4 %copy-start.12 = (s32[2]{0:T(128)}, s32[2]{0:T(128)S(1)}, u32[]{:S(2)}) copy-start(s32[2]{0:T(128)S(1)} %pad_add_fusion.pos_ref) | copy-start | bytes 28
  149.0 1.0 copy-start.6
  150.0 36.5 %copy-start.11 = (f32[512]{0:T(512)S(1)}, f32[512]{0:T(512)}, u32[]{:S(2)}) copy-start(f32[512]{0:T(512)} %param.19) | copy-start | bytes 6148
  153.5 0.6 copy-start.7
  154.1 0.6 copy-start.10
  154.7 3.7 %collective-permute-start.8 = (f32[32,128]{1,0:T(8,128)S(1)}, f32[32,128]{1,0:T(8,128)S(1)}, u32[]{:S(2)}, u32[]{:S(2)}) collective-permute-start(f32[32,128]{1,0:T(8,128)S(1)} %get-tuple-element.25), channel_id=1, source_target_pairs={{0,16},{16,0},{32,48},{48,32},{64,80},{80,64},{96,112},{112,96},{1... | collective-permute-start | bytes 49160 | tf_op jit(solution)/shard_map/ppermute | solution.py:503
  158.4 0.6 copy-start.14
  161.5 4.3 %collective-permute-start.10 = (bf16[8,128]{1,0:T(8,128)(2,1)S(1)}, bf16[8,128]{1,0:T(8,128)(2,1)S(1)}, u32[]{:S(2)}, u32[]{:S(2)}) collective-permute-start(bf16[8,128]{1,0:T(8,128)(2,1)S(1)} %get-tuple-element.30), channel_id=1, source_target_pairs={{1,0},{2,1},{3,2},{4,3},{5,4},{6,5},{7,6},{8,7},{9,8},{10,9},{11,1... | collective-permute-start | bytes 6152 | tf_op jit(solution)/shard_map/ppermute | solution.py:507
  163.4 8.5 %collective-permute-start.9 = (bf16[8,128]{1,0:T(8,128)(2,1)S(1)}, bf16[8,128]{1,0:T(8,128)(2,1)S(1)}, u32[]{:S(2)}, u32[]{:S(2)}) collective-permute-start(bf16[8,128]{1,0:T(8,128)(2,1)S(1)} %get-tuple-element.29), channel_id=1, source_target_pairs={{0,1},{1,2},{2,3},{3,4},{4,5},{5,6},{6,7},{7,8},{8,9},{9,10},{10,1... | collective-permute-start | bytes 6152 | tf_op jit(solution)/shard_map/ppermute | solution.py:506
  173.3 13.2 %all-to-all-start.4 = ((bf16[16,32,128]{2,1,0:T(8,128)(2,1)}), bf16[16,32,128]{2,1,0:T(8,128)(2,1)S(1)}, u32[]{:S(2)}, u32[]{:S(2)}) async-start(bf16[16,32,128]{2,1,0:T(8,128)(2,1)} %broadcast_in_dim.2), calls=%async_computation.4 | async-start | bytes 262144 | tf_op jit(solution)/shard_map/all_to_all | solution.py:509
  186.5 1.2 copy-start.3
  187.7 1.0 copy-start.5
Sparse Core Ops, SparseCore 0:
  37.9 59.1 all-gather.1
